TPU v7x, 768 devices: a whole 4x8x12 slice. The times are simulated.
768 devices in a mesh: cell: 16 (over y, core), vel: 48 (over x, z).
Axes of the slice: x: 4, y: 8, z: 12, core: 2. Of those that a mesh axis runs over, the one named last changes fastest.
Arguments:
- distribution: float32 [3072, 16, 384], P('vel', 'cell'), may hold values from 0.1 to 2
- gain_left: float32 [2, 3072], replicated, may hold values from -3 to 3
- gain_right: float32 [2, 3072], replicated, may hold values from -3 to 3
- loss_kernel: float32 [3072], replicated, may hold values from 0.1 to 1.5
- wall_cell: int32 [16, 48, 8], P('cell', 'vel'), may hold values from 0 to 7
- wall_count: int32 [16, 48], P('cell', 'vel'), may hold values from 0 to 8, as said below
- wall_panel: int32 [16, 48, 8], P('cell', 'vel'), may hold values from 0 to 3071, as said below
Outputs:
- final_distribution: float32 [3072, 16, 384], P('vel', 'cell')
- panel_loads: float32 [4, 3072], P(None, ('cell', 'vel'))
Inputs may be any that keep to these rules, and one draw needn't show every extreme that they name: `wall_count`: slots from the count on are padding; some column uses all 8 slots. The panel of a slot in column (x, y) satisfies (wall_panel // 4) % 48 == y; padding slots hold valid panel numbers.
All inputs are finite; a program needn't handle non-finite values.
Results may differ from a plain program's by a relative error of at most 0.0001.
Values sent between devices are 32-bit elements; how exact they have to be, the bound alone decides.
A program may use at most 32 MiB of HBM per device.

v0:
```python
import functools
import math

import jax
import jax.numpy as jnp
import ml_dtypes
import numpy as np
from jax import lax
from jax.experimental import pallas as pl
from jax.experimental.pallas import tpu as pltpu
from jax.sharding import PartitionSpec as P

NVY = 16
NVZ = 12
PLANE = NVY * NVZ
HALF = PLANE // 2
KEPT = NVZ // 2 + 1
KERNELS = 5
DIRS = 2
MOMENTS = 4
STEPS = 3
NZ = 8
WALL_SLOTS = 8
PANEL_DEV = 4
LOCAL_V = 64
PARTS = PLANE // LOCAL_V
LANES = 128

SPACING = 0.5
COURANT = 0.09
COLLISION_STEP = 0.3

MESH = pl.DeviceIdType.MESH


def split(values):
    high = values.astype(ml_dtypes.bfloat16)
    low = (values - high.astype(np.float64)).astype(ml_dtypes.bfloat16)
    return high, low


def plane_matrices():
    table = np.zeros((2 * LANES, 2 * LANES))
    for point in range(PLANE):
        b, c = divmod(point, NVZ)
        row = b // (NVY // 2) * LANES + point % HALF
        for kb in range(NVY):
            for kc in range(KEPT):
                angle = 2.0 * math.pi * ((b * kb % NVY) / NVY + (c * kc % NVZ) / NVZ)
                table[row, kb * KEPT + kc] = math.cos(angle)
                table[row, LANES + kb * KEPT + kc] = -math.sin(angle)
    high, low = split(table)
    return np.concatenate([high, low, high.T, low.T], axis=0)


def lane_tables():
    lane = np.arange(LANES)
    used = (lane < HALF).astype(np.float64)
    vz = (2 * (lane % NVZ) - (NVZ - 1)) * 0.5 * SPACING * used
    vy = [(2 * (lane // NVZ + h * NVY // 2) - (NVY - 1)) * 0.5 * SPACING * used for h in (0, 1)]
    z = np.arange(NZ)[:, None]
    rows = []
    for h in (0, 1):
        rows.append(1.0 - COURANT * (np.abs(vy[h]) + np.abs(vz)) + 0.0 * z)
    for h in (0, 1):
        rows.append(COURANT * np.abs(vy[h]) + 0.0 * z)
    rows.append(COURANT * np.maximum(vz, 0.0) * (z > 0))
    rows.append(COURANT * np.maximum(-vz, 0.0) * (z < NZ - 1))
    cube = SPACING**3
    rows.append(cube * vy[0] + 0.0 * z)
    rows.append(cube * vy[1] + 0.0 * z)
    rows.append(cube * vz + 0.0 * z)
    rows.append(cube * (vy[0] ** 2 + vz**2) + 0.0 * z)
    rows.append(cube * (vy[1] ** 2 + vz**2) + 0.0 * z)
    return np.stack(rows).astype(np.float32)


def fourier(real, imag, sign):
    count = len(real)
    if count == 1:
        return real, imag
    even_r, even_i = fourier(real[::2], imag[::2], sign)
    odd_r, odd_i = fourier(real[1::2], imag[1::2], sign)
    out_r, out_i = [None] * count, [None] * count
    half = count // 2
    for k in range(half):
        r, i = odd_r[k], odd_i[k]
        if k == 0:
            pass
        elif 4 * k == count:
            r, i = (-i, r) if sign > 0 else (i, -r)
        else:
            cos = math.cos(2.0 * math.pi * k / count)
            sin = sign * math.sin(2.0 * math.pi * k / count)
            if 8 * k == count or 8 * k == 3 * count:
                size = math.sqrt(0.5)
                up, across = cos / abs(cos), sin / abs(sin)
                first = r - i if up == across else r + i
                second = r + i if up == across else (i - r)
                if up > 0:
                    r, i = (first * size, second * size)
                else:
                    r, i = (first * -size, second * -size)
            else:
                r, i = r * cos - i * sin, r * sin + i * cos
        out_r[k], out_i[k] = even_r[k] + r, even_i[k] + i
        out_r[k + half], out_i[k + half] = even_r[k] - r, even_i[k] - i
    return out_r, out_i


def exact_dot(values, high, low):
    top = values.astype(jnp.bfloat16)
    rest = (values - top.astype(jnp.float32)).astype(jnp.bfloat16)
    dot = functools.partial(jnp.dot, preferred_element_type=jnp.float32)
    return dot(top, high) + (dot(rest, high) + dot(top, low))


def kernel(
    cells, columns,
    x_in, mats_in, sym_in, lanes_in, wall_cell_in, wall_count_in, wall_panel_in,
    out, loads,
    x_v, mats, sym, lanes, wall_cell, wall_count, wall_panel,
    packed, arrived, packed_back, arrived_back, state, halo_x, halo_y,
    spec, back, mine, others,
    in_sems, halo_send, halo_recv, swap_send, swap_recv, load_send, load_recv,
):
    nvx = columns // PARTS
    mid = nvx // 2
    me_c = lax.axis_index("cell")
    me_v = lax.axis_index("vel")

    pairs = [
        (x_in, x_v), (mats_in, mats), (sym_in, sym), (lanes_in, lanes),
        (wall_cell_in, wall_cell), (wall_count_in, wall_count), (wall_panel_in, wall_panel),
    ]
    loads_in = [pltpu.make_async_copy(src, dst, in_sems.at[n]) for n, (src, dst) in enumerate(pairs)]
    for copy in loads_in:
        copy.start()

    barrier = pltpu.get_barrier_semaphore()

    def greet_column(j, carry):
        to = lax.rem(me_v + j, columns)
        pl.semaphore_signal(barrier, inc=1, device_id=(me_c, to), device_id_type=MESH)
        return carry

    def greet_row(j, carry):
        to = lax.rem(me_c + j, cells)
        pl.semaphore_signal(barrier, inc=1, device_id=(to, me_v), device_id_type=MESH)
        return carry

    lax.fori_loop(1, columns, greet_column, 0)
    lax.fori_loop(1, cells, greet_row, 0)

    has_low_x, has_high_x = me_c > 0, me_c < cells - 1
    has_low_y, has_high_y = me_v > 0, me_v < columns - 1

    @pl.when(jnp.logical_not(has_low_x))
    def _():
        halo_x[:, :, mid:] = jnp.zeros((STEPS, 2, mid, NZ, LANES), jnp.float32)

    @pl.when(jnp.logical_not(has_high_x))
    def _():
        halo_x[:, :, :mid] = jnp.zeros((STEPS, 2, mid, NZ, LANES), jnp.float32)

    @pl.when(jnp.logical_not(has_low_y))
    def _():
        halo_y[:, 1] = jnp.zeros((STEPS, nvx, NZ, LANES), jnp.float32)

    @pl.when(jnp.logical_not(has_high_y))
    def _():
        halo_y[:, 0] = jnp.zeros((STEPS, nvx, NZ, LANES), jnp.float32)

    loads_in[0].wait()
    width = NZ * columns
    for start in range(0, width, LANES):
        stop = min(start + LANES, width)
        tile = x_v[:, 0, start:stop]
        shifted = jnp.concatenate([tile[:, NZ // 2 :], tile[:, : NZ // 2]], axis=1)
        turned = jnp.transpose(jnp.concatenate([tile, shifted], axis=0))
        turned = turned.reshape((stop - start) // NZ, NZ, LANES)
        packed[start // NZ : stop // NZ] = turned[:, : NZ // 2]
    arrived[pl.ds(me_v, 1)] = packed[pl.ds(me_v, 1)]

    pl.semaphore_wait(barrier, columns - 1 + cells - 1)

    def exchange(source, target, which):
        def send(j, carry):
            to = lax.rem(me_v + j, columns)
            pltpu.make_async_remote_copy(
                src_ref=source.at[to],
                dst_ref=target.at[me_v],
                send_sem=swap_send.at[which],
                recv_sem=swap_recv.at[which],
                device_id=(me_c, to),
                device_id_type=MESH,
            ).start()
            return carry

        lax.fori_loop(1, columns, send, 0)

    def arrivals(target, which):
        rest = target.at[pl.ds(0, columns - 1)]
        pltpu.make_async_copy(rest, rest, swap_recv.at[which]).wait()

    def departures(source, which):
        rest = source.at[pl.ds(0, columns - 1)]
        pltpu.make_async_copy(rest, rest, swap_send.at[which]).wait()

    exchange(packed, arrived, 0)
    for copy in loads_in[1:]:
        copy.wait()
    arrivals(arrived, 0)

    lane = lax.broadcasted_iota(jnp.int32, (1, 1, LANES), 2)
    used = lane < HALF
    quarter = LOCAL_V // 2

    def turn(values, by):
        return pltpu.roll(values, by, values.ndim - 1)

    blocks = arrived[...].reshape(nvx, PARTS, NZ // 2, LANES)
    wide = []
    for part in range(PARTS):
        block = blocks[:, part]
        wide.append(jnp.concatenate([block, turn(block, LOCAL_V)], axis=1))
    state[0, 0] = jnp.where(lane < LOCAL_V, wide[0], jnp.where(used, turn(wide[1], LOCAL_V), 0.0))
    state[0, 1] = jnp.where(
        lane < quarter, turn(wide[1], LANES - quarter), jnp.where(used, turn(wide[2], quarter), 0.0)
    )

    def halo_copies(step):
        routes = [
            (state.at[step, :, pl.ds(mid, mid)], halo_x.at[step, :, pl.ds(mid, mid)], (me_c + 1, me_v)),
            (state.at[step, :, pl.ds(0, mid)], halo_x.at[step, :, pl.ds(0, mid)], (me_c - 1, me_v)),
            (state.at[step, 1], halo_y.at[step, 1], (me_c, me_v + 1)),
            (state.at[step, 0], halo_y.at[step, 0], (me_c, me_v - 1)),
        ]
        return [
            pltpu.make_async_remote_copy(
                src_ref=src,
                dst_ref=dst,
                send_sem=halo_send.at[n, step],
                recv_sem=halo_recv.at[n, step],
                device_id=to,
                device_id_type=MESH,
            )
            for n, (src, dst, to) in enumerate(routes)
        ]

    sends = [has_high_x, has_low_x, has_high_y, has_low_y]
    receives = [has_low_x, has_high_x, has_low_y, has_high_y]

    def speed_x(a):
        return (2 * a - (nvx - 1)) * 0.5 * SPACING

    def advance(step, carry):
        copies = halo_copies(step)
        for copy, present in zip(copies, sends):
            pl.when(present)(copy.start)

        own = []
        for h in (0, 1):
            here = state[step, h]
            own.append(
                here * lanes[h]
                + pltpu.roll(here, 1, 1) * lanes[4]
                + pltpu.roll(here, NZ - 1, 1) * lanes[5]
            )

        for copy, present in zip(copies, receives):
            pl.when(present)(copy.wait_recv)

        moved = []
        for h in (0, 1):
            side = []
            for a in range(nvx):
                weight = COURANT * abs(speed_x(a))
                side.append(own[h][a] + (halo_x[step, h, a] - state[step, h, a]) * weight)
            moved.append(jnp.stack(side) + halo_y[step, h] * lanes[2 + h])
        rows = jnp.concatenate([side.reshape(nvx * NZ, LANES) for side in moved], axis=1)

        span = 2 * LANES
        plane = exact_dot(rows, mats[:span], mats[span : 2 * span]).reshape(nvx, NZ, span)
        real, imag = fourier(
            [plane[a, :, :LANES] for a in range(nvx)], [plane[a, :, LANES:] for a in range(nvx)], -1
        )
        spec[0] = jnp.stack(real)
        spec[1] = jnp.stack(imag)

        def weigh(w, carry):
            gains = [sym[w, pl.ds(a, 1), :] for a in range(nvx)]
            real, imag = fourier(
                [spec[0, a] * gains[a] for a in range(nvx)], [spec[1, a] * gains[a] for a in range(nvx)], 1
            )
            line = jnp.concatenate(
                [jnp.concatenate(real, axis=0), jnp.concatenate(imag, axis=0)], axis=1
            )
            back[w] = exact_dot(line, mats[2 * span : 3 * span], mats[3 * span :])
            return carry

        lax.fori_loop(0, KERNELS, weigh, 0, unroll=True)
        change = back[0] * back[2] + back[1] * back[3] - rows * back[4]
        after = rows + COLLISION_STEP * change
        for h in (0, 1):
            state[step + 1, h] = after[:, h * LANES : (h + 1) * LANES].reshape(nvx, NZ, LANES)
        return carry

    lax.fori_loop(0, STEPS, advance, 0)

    low, high = state[STEPS, 0], state[STEPS, 1]
    parts = [
        low,
        jnp.where(lane < quarter, turn(low, LOCAL_V), turn(high, quarter)),
        turn(high, LANES - quarter),
    ]
    stacked = [
        jnp.where(lane < LOCAL_V, part[:, : NZ // 2], turn(part, LOCAL_V)[:, NZ // 2 :]) for part in parts
    ]
    packed_back[...] = jnp.stack(stacked, axis=1).reshape(columns, NZ // 2, LANES)
    exchange(packed_back, arrived_back, 1)
    arrived_back[pl.ds(me_v, 1)] = packed_back[pl.ds(me_v, 1)]

    both = low + high
    sums_low, sums_high = jnp.sum(low, axis=0), jnp.sum(high, axis=0)
    along, squared = 0.0, 0.0
    for a in range(nvx):
        along = along + both[a] * (SPACING**3 * speed_x(a))
        squared = squared + both[a] * (SPACING**3 * speed_x(a) ** 2)
    totals = [
        along,
        sums_low * lanes[6] + sums_high * lanes[7],
        (sums_low + sums_high) * lanes[8],
        squared + sums_low * lanes[9] + sums_high * lanes[10],
    ]
    depth = lax.broadcasted_iota(jnp.int32, (NZ, LANES), 0)
    slot = lax.broadcasted_iota(jnp.int32, (NZ, LANES), 1)
    uses = jnp.zeros((NZ, LANES), jnp.float32)
    per_owner = PANEL_DEV * columns
    for n in range(WALL_SLOTS):
        panel = wall_panel[0, 0, n]
        target = panel // per_owner * PANEL_DEV + lax.rem(panel, PANEL_DEV)
        target = jnp.where(n < wall_count[0, 0], target, -1)
        hit = jnp.logical_and(depth == wall_cell[0, 0, n], slot == target)
        uses = uses + jnp.where(hit, 1.0, 0.0)
    shares = [
        jnp.sum(jnp.sum(total, axis=1, keepdims=True) * uses, axis=0, keepdims=True) for total in totals
    ]
    shares.append(jnp.zeros((NZ - MOMENTS, LANES), jnp.float32))
    share = jnp.concatenate(shares, axis=0)
    mine[...] = share
    others[pl.ds(me_c, 1)] = share[None]

    def give(j, carry):
        to = lax.rem(me_c + j, cells)
        pltpu.make_async_remote_copy(
            src_ref=mine,
            dst_ref=others.at[me_c],
            send_sem=load_send,
            recv_sem=load_recv,
            device_id=(to, me_v),
            device_id_type=MESH,
        ).start()
        return carry

    lax.fori_loop(1, cells, give, 0)

    rest = others.at[pl.ds(0, cells - 1)]
    pltpu.make_async_copy(rest, rest, load_recv).wait()
    summed = jnp.sum(others[...], axis=0)
    picked = slot - PANEL_DEV * me_c
    columns_out = [
        jnp.sum(jnp.where(picked == k, summed, 0.0), axis=1, keepdims=True) for k in range(PANEL_DEV)
    ]
    loads[...] = jnp.concatenate(columns_out, axis=1)[:MOMENTS]

    arrivals(arrived_back, 1)
    for start in range(0, columns, LANES // NZ):
        stop = min(start + LANES // NZ, columns)
        block = arrived_back[start:stop]
        tall = jnp.concatenate([block, turn(block, LOCAL_V)], axis=1).reshape((stop - start) * NZ, LANES)
        out[:, start * NZ : stop * NZ] = jnp.transpose(tall)[:LOCAL_V]

    departures(packed, 0)
    departures(packed_back, 1)
    pltpu.make_async_copy(rest, rest, load_send).wait()

    def finish(step, carry):
        for copy, present in zip(halo_copies(step), sends):
            pl.when(present)(copy.wait_send)
        return carry

    lax.fori_loop(0, STEPS, finish, 0)


def even_weights(gain_left, gain_right, loss_kernel):
    kernels = jnp.concatenate([gain_left, gain_right, loss_kernel[None]], axis=0)
    full = kernels.reshape(KERNELS, -1, NVY, NVZ)
    mirrored = full
    for axis in (1, 2, 3):
        mirrored = jnp.roll(jnp.flip(mirrored, axis), 1, axis)
    count = full.shape[1] * PLANE
    twice = np.full(KEPT, 2.0)
    twice[0] = twice[-1] = 1.0
    scale = jnp.asarray((0.5 * twice / count).astype(np.float32))
    kept = (full + mirrored)[..., :KEPT] * scale
    flat = kept.reshape(KERNELS, full.shape[1], NVY * KEPT)
    return jnp.pad(flat, ((0, 0), (0, 0), (0, LANES - NVY * KEPT)))


def per_device(cells, columns, distribution, gain_left, gain_right, loss_kernel, wall_cell, wall_count, wall_panel):
    nvx = columns // PARTS
    local, _, width = distribution.shape
    f32 = jnp.float32
    sym = even_weights(gain_left, gain_right, loss_kernel)
    mats = jnp.asarray(plane_matrices())
    tables = jnp.asarray(lane_tables())
    anywhere = pl.BlockSpec(memory_space=pl.ANY)
    in_vmem = pl.BlockSpec(memory_space=pltpu.VMEM)
    dma = pltpu.SemaphoreType.DMA
    out, loads = pl.pallas_call(
        functools.partial(kernel, cells, columns),
        out_shape=(
            jax.ShapeDtypeStruct((local, width), f32),
            jax.ShapeDtypeStruct((MOMENTS, PANEL_DEV), f32),
        ),
        in_specs=[anywhere] * 7,
        out_specs=(in_vmem, in_vmem),
        scratch_shapes=[
            pltpu.VMEM(distribution.shape, f32),
            pltpu.VMEM(mats.shape, jnp.bfloat16),
            pltpu.VMEM(sym.shape, f32),
            pltpu.VMEM(tables.shape, f32),
            pltpu.SMEM(wall_cell.shape, jnp.int32),
            pltpu.SMEM(wall_count.shape, jnp.int32),
            pltpu.SMEM(wall_panel.shape, jnp.int32),
            pltpu.VMEM((columns, NZ // 2, LANES), f32),
            pltpu.VMEM((columns, NZ // 2, LANES), f32),
            pltpu.VMEM((columns, NZ // 2, LANES), f32),
            pltpu.VMEM((columns, NZ // 2, LANES), f32),
            pltpu.VMEM((STEPS + 1, 2, nvx, NZ, LANES), f32),
            pltpu.VMEM((STEPS, 2, nvx, NZ, LANES), f32),
            pltpu.VMEM((STEPS, 2, nvx, NZ, LANES), f32),
            pltpu.VMEM((2, nvx, NZ, LANES), f32),
            pltpu.VMEM((KERNELS, nvx * NZ, 2 * LANES), f32),
            pltpu.VMEM((NZ, LANES), f32),
            pltpu.VMEM((cells, NZ, LANES), f32),
            dma((7,)),
            dma((4, STEPS)),
            dma((4, STEPS)),
            dma((2,)),
            dma((2,)),
            dma,
            dma,
        ],
        compiler_params=pltpu.CompilerParams(
            collective_id=0, has_side_effects=True, vmem_limit_bytes=32 * 1024 * 1024
        ),
        cost_estimate=pl.CostEstimate(flops=1_000_000_000, bytes_accessed=2_000_000, transcendentals=0),
        name="collide",
    )(distribution, mats, sym, tables, wall_cell, wall_count, wall_panel)
    return out.reshape(local, 1, width), loads


def solution(mesh):
    placed = (
        P("vel", "cell", None),
        P(),
        P(),
        P(),
        P("cell", "vel", None),
        P("cell", "vel"),
        P("cell", "vel", None),
    )
    return jax.shard_map(
        functools.partial(per_device, mesh.shape["cell"], mesh.shape["vel"]),
        mesh=mesh,
        in_specs=placed,
        out_specs=(P("vel", "cell", None), P(None, ("cell", "vel"))),
        check_vma=False,
    )
```

profile of v0, /device:TPU:3, one launch (start us, length us, event | category | flops | bytes accessed | tf_op | source)
XLA Modules:
  0.0 60.6 jit_solution(3694459146407806738)
XLA Ops:
  0.6 1.0 %concatenate.22 = f32[2,16,16,12]{3,2,1,0:T(8,128)S(1)} reshape(f32[2,3072]{1,0:T(2,128)} %param.11) | data formatting | bytes 49152 | tf_op jit(solution)/shard_map/concatenate | solution.py:397
  1.7 0.0 copy-start.5
  1.7 0.3 copy.16
  1.9 0.5 copy-done.5
  2.4 0.3 concatenate.23
  2.7 0.0 copy-start.6
  2.7 0.3 copy.17
  3.0 0.4 copy-done.6
  3.4 0.1 concatenate.24
  3.5 0.2 copy.18
  3.7 0.1 pad_maximum_fusion.1
  3.8 0.2 slice.41
  4.0 0.1 slice_maximum_fusion
  4.1 0.3 pad_maximum_fusion
  4.4 0.2 slice.44
  4.6 0.2 pad_maximum_fusion.2
  4.7 0.0 copy-start.7
  4.8 0.6 %copy-done.7 = f32[7]{0:T(128)S(1)} copy-done((f32[7]{0:T(128)S(1)}, f32[7]{0:T(128)}, u32[]{:S(2)}) %copy-start.7) | copy-done | bytes 52
  5.4 0.1 fusion
  5.5 0.5 copy.22
  6.1 0.0 copy-start.3
  6.1 0.3 reshape.18
  6.4 0.0 copy-start.1
  6.4 0.0 copy-start.2
  7.1 0.0 copy-done
  7.1 0.1 copy-done.3
  7.2 0.1 copy-done.4
  7.2 0.0 copy-done.1
  7.2 0.0 copy-done.2
  7.2 52.1 %collide.1 = (f32[64,384]{1,0:T(8,128)S(1)}, f32[4,4]{1,0:T(4,128)S(1)}) custom-call(f32[64,1,384]{2,1,0:T(1,128)S(1)} %copy-done, bf16[1024,256]{1,0:T(8,128)(2,1)S(1)} %copy-done.3, f32[5,16,128]{2,1,0:T(8,128)S(1)} %pad.4.sym_in, f32[11,8,128]{2,1,0:T(8,128)S(1)} %copy-done.4, s32[1,1,8]{2,1,0:T(1,128)S(1)} %copy-done.1, s32[1,1]{1,0:T(1,128)S(6)} %copy.25.wall_count_in, ...), custom_call_target="tpu_custom_call" | custom-call | flops 1000000000 | bytes 2000000 | tf_op jit(solution)/shard_map/collide/pallas_call | solution.py:421
  59.3 0.7 %copy.21 = f32[64,1,384]{2,1,0:T(1,128)} copy(f32[64,1,384]{2,0,1:T(8,128)S(1)} %bitcast.3) | data formatting | bytes 196608
  60.1 0.6 copy.26
  (6 shorter events, 0.1 us)
Async XLA Ops:
  1.7 0.7 %copy-start.5 = (f32[2,3072]{1,0:T(2,128)S(1)}, f32[2,3072]{1,0:T(2,128)}, u32[]{:S(2)}) copy-start(f32[2,3072]{1,0:T(2,128)} %param.12) | copy-start | bytes 73732
  2.7 0.7 %copy-start.6 = (f32[3072]{0:T(1024)S(1)}, f32[3072]{0:T(1024)}, u32[]{:S(2)}) copy-start(f32[3072]{0:T(1024)} %param.13) | copy-start | bytes 36868
  4.7 0.7 %copy-start.7 = (f32[7]{0:T(128)S(1)}, f32[7]{0:T(128)}, u32[]{:S(2)}) copy-start(f32[7]{0:T(128)} %constant.9.clone) | copy-start | bytes 88
  6.1 1.0 %copy-start = (f32[64,1,384]{2,1,0:T(1,128)S(1)}, f32[64,1,384]{2,1,0:T(1,128)}, u32[]{:S(2)}) copy-start(f32[64,1,384]{2,1,0:T(1,128)} %x_in.1) | copy-start | bytes 294916
  6.1 1.1 %copy-start.3 = (bf16[1024,256]{1,0:T(8,128)(2,1)S(1)}, bf16[1024,256]{1,0:T(8,128)(2,1)}, u32[]{:S(2)}) copy-start(bf16[1024,256]{1,0:T(8,128)(2,1)} %constant.10.clone.mats_in) | copy-start | bytes 1572868
  6.4 0.8 %copy-start.4 = (f32[11,8,128]{2,1,0:T(8,128)S(1)}, f32[11,8,128]{2,1,0:T(8,128)}, u32[]{:S(2)}) copy-start(f32[11,8,128]{2,1,0:T(8,128)} %constant.11.clone.lanes_in) | copy-start | bytes 135172
  6.4 0.8 %copy-start.1 = (s32[1,1,8]{2,1,0:T(1,128)S(1)}, s32[1,1,8]{2,1,0:T(1,128)}, u32[]{:S(2)}) copy-start(s32[1,1,8]{2,1,0:T(1,128)} %wall_cell_in.1) | copy-start | bytes 100
  6.4 0.8 %copy-start.2 = (s32[1,1,8]{2,1,0:T(1,128)S(1)}, s32[1,1,8]{2,1,0:T(1,128)}, u32[]{:S(2)}) copy-start(s32[1,1,8]{2,1,0:T(1,128)} %wall_panel_in.1) | copy-start | bytes 100
where the time goes:
time: 61 us; the launch traced here: 60.6 us
  Pallas kernels  52.1 us (85%)
  local copies, waits for them, and re-layouts  6.39 us (10%)
  between operations  1.46 us (2%)
  other arithmetic  0.69 us (1%)
    pallas_call x1, Pallas kernels, per_device(): pl.pallas_call(functools.partial(kernel, cells, columns), out_shape=(jax....  52.1 us
    unnamed x18, local copies, waits for them, and re-layouts  2.95 us
    concatenate x6, local copies, waits for them, and re-layouts, even_weights(): jnp.concatenate([gain_left, gain_right, loss_kernel[None]], axis=0)  2.16 us

commit v1 on v0

--- a/solution.py
+++ b/solution.py
@@ -25,6 +25,7 @@
 LOCAL_V = 64
 PARTS = PLANE // LOCAL_V
 LANES = 128
+VMEM_LIMIT = 60 * 1024 * 1024
 
 SPACING = 0.5
 COURANT = 0.09
@@ -51,6 +52,20 @@
                 table[row, LANES + kb * KEPT + kc] = -math.sin(angle)
     high, low = split(table)
     return np.concatenate([high, low, high.T, low.T], axis=0)
+
+
+def weight_selectors():
+    table = np.zeros((2 * PLANE, 4 * LANES))
+    for kb in range(NVY):
+        for kc in range(KEPT):
+            share = 0.5 if kc in (0, KEPT - 1) else 1.0
+            column = kb * KEPT + kc
+            there = kb * NVZ + kc
+            mirror = -kb % NVY * NVZ + -kc % NVZ
+            for half in (0, 1):
+                table[half * PLANE + there, half * LANES + column] = share
+                table[half * PLANE + mirror, (2 + half) * LANES + column] = share
+    return table.astype(ml_dtypes.bfloat16)
 
 
 def lane_tables():
@@ -117,21 +132,44 @@
 
 def kernel(
     cells, columns,
-    x_in, mats_in, sym_in, lanes_in, wall_cell_in, wall_count_in, wall_panel_in,
+    x_in, wall_cell_in, wall_count_in, wall_panel_in, left_in, right_in, loss_in, picks_in, mats_in, lanes_in,
     out, loads,
-    x_v, mats, sym, lanes, wall_cell, wall_count, wall_panel,
+    x_v, wall_cell, wall_count, wall_panel, left, right, loss, picks, mats, lanes,
     packed, arrived, packed_back, arrived_back, state, halo_x, halo_y,
-    spec, back, mine, others,
-    in_sems, halo_send, halo_recv, swap_send, swap_recv, load_send, load_recv,
+    planes, sym, spec, back, my_uses, uses, mine, others,
+    in_sems, halo_send, halo_recv, swap_send, swap_recv, load_send, load_recv, uses_send, uses_recv,
 ):
     nvx = columns // PARTS
     mid = nvx // 2
     me_c = lax.axis_index("cell")
     me_v = lax.axis_index("vel")
 
+    lines = 4 if columns % 4 == 0 else 2
+    ring = columns // lines
+
+    def owner_of(column):
+        line, place = column // ring, lax.rem(column, ring)
+        return line * ring + lax.rem(place + 1 - line + ring, ring)
+
+    def column_of(device):
+        line, place = device // ring, lax.rem(device, ring)
+        return line * ring + lax.rem(place - 1 + line + ring, ring)
+
+    me_y = column_of(me_v)
+    my_owner = owner_of(me_v)
+    line, place = me_v // ring, lax.rem(me_v, ring)
+
+    def descending(n, count):
+        half = (n + 1) // 2
+        return lax.rem(count // 2 + jnp.where(lax.rem(n, 2) == 1, half, -half), count)
+
+    def partner(j):
+        there = lax.rem(place + descending(j // lines, ring), ring)
+        return lax.rem(line + descending(lax.rem(j, lines), lines), lines) * ring + there
+
     pairs = [
-        (x_in, x_v), (mats_in, mats), (sym_in, sym), (lanes_in, lanes),
-        (wall_cell_in, wall_cell), (wall_count_in, wall_count), (wall_panel_in, wall_panel),
+        (x_in, x_v), (wall_cell_in, wall_cell), (wall_count_in, wall_count), (wall_panel_in, wall_panel),
+        (left_in, left), (right_in, right), (loss_in, loss), (picks_in, picks), (mats_in, mats), (lanes_in, lanes),
     ]
     loads_in = [pltpu.make_async_copy(src, dst, in_sems.at[n]) for n, (src, dst) in enumerate(pairs)]
     for copy in loads_in:
@@ -140,36 +178,28 @@
     barrier = pltpu.get_barrier_semaphore()
 
     def greet_column(j, carry):
-        to = lax.rem(me_v + j, columns)
-        pl.semaphore_signal(barrier, inc=1, device_id=(me_c, to), device_id_type=MESH)
+        pl.semaphore_signal(barrier, inc=1, device_id=(me_c, partner(j)), device_id_type=MESH)
         return carry
 
     def greet_row(j, carry):
         to = lax.rem(me_c + j, cells)
-        pl.semaphore_signal(barrier, inc=1, device_id=(to, me_v), device_id_type=MESH)
+        pl.semaphore_signal(barrier, inc=1, device_id=(to, my_owner), device_id_type=MESH)
         return carry
 
-    lax.fori_loop(1, columns, greet_column, 0)
+    has_low_x, has_high_x = me_c > 0, me_c < cells - 1
+    has_low_y, has_high_y = me_y > 0, me_y < columns - 1
+    moved_home = my_owner != me_v
+    greetings = [(jnp.logical_and(moved_home, has_low_x), -1), (jnp.logical_and(moved_home, has_high_x), 1)]
+
+    lax.fori_loop(0, columns - 1, greet_column, 0)
     lax.fori_loop(1, cells, greet_row, 0)
-
-    has_low_x, has_high_x = me_c > 0, me_c < cells - 1
-    has_low_y, has_high_y = me_v > 0, me_v < columns - 1
-
-    @pl.when(jnp.logical_not(has_low_x))
-    def _():
-        halo_x[:, :, mid:] = jnp.zeros((STEPS, 2, mid, NZ, LANES), jnp.float32)
-
-    @pl.when(jnp.logical_not(has_high_x))
-    def _():
-        halo_x[:, :, :mid] = jnp.zeros((STEPS, 2, mid, NZ, LANES), jnp.float32)
-
-    @pl.when(jnp.logical_not(has_low_y))
-    def _():
-        halo_y[:, 1] = jnp.zeros((STEPS, nvx, NZ, LANES), jnp.float32)
-
-    @pl.when(jnp.logical_not(has_high_y))
-    def _():
-        halo_y[:, 0] = jnp.zeros((STEPS, nvx, NZ, LANES), jnp.float32)
+    greeted = columns - 1 + cells - 1
+    for present, way in greetings:
+        greeted = greeted + jnp.where(present, 1, 0)
+
+        @pl.when(present)
+        def _():
+            pl.semaphore_signal(barrier, inc=1, device_id=(me_c + way, me_v), device_id_type=MESH)
 
     loads_in[0].wait()
     width = NZ * columns
@@ -180,16 +210,34 @@
         turned = jnp.transpose(jnp.concatenate([tile, shifted], axis=0))
         turned = turned.reshape((stop - start) // NZ, NZ, LANES)
         packed[start // NZ : stop // NZ] = turned[:, : NZ // 2]
-    arrived[pl.ds(me_v, 1)] = packed[pl.ds(me_v, 1)]
-
-    pl.semaphore_wait(barrier, columns - 1 + cells - 1)
-
-    def exchange(source, target, which):
+    arrived[pl.ds(me_v, 1)] = packed[pl.ds(me_y, 1)]
+
+    depth = lax.broadcasted_iota(jnp.int32, (NZ, LANES), 0)
+    slot = lax.broadcasted_iota(jnp.int32, (NZ, LANES), 1)
+    for copy in loads_in[1:4]:
+        copy.wait()
+    counted = jnp.zeros((NZ, LANES), jnp.float32)
+    per_owner = PANEL_DEV * columns
+    for n in range(WALL_SLOTS):
+        panel = wall_panel[0, 0, n]
+        target = panel // per_owner * PANEL_DEV + lax.rem(panel, PANEL_DEV)
+        target = jnp.where(n < wall_count[0, 0], target, -1)
+        hit = jnp.logical_and(depth == wall_cell[0, 0, n], slot == target)
+        counted = counted + jnp.where(hit, 1.0, 0.0)
+    my_uses[...] = counted
+
+    @pl.when(jnp.logical_not(moved_home))
+    def _():
+        uses[...] = counted
+
+    pl.semaphore_wait(barrier, greeted)
+
+    def exchange(source, target, which, source_slot, target_slot):
         def send(j, carry):
-            to = lax.rem(me_v + j, columns)
+            to = partner(j)
             pltpu.make_async_remote_copy(
-                src_ref=source.at[to],
-                dst_ref=target.at[me_v],
+                src_ref=source.at[source_slot(to)],
+                dst_ref=target.at[target_slot],
                 send_sem=swap_send.at[which],
                 recv_sem=swap_recv.at[which],
                 device_id=(me_c, to),
@@ -197,7 +245,7 @@
             ).start()
             return carry
 
-        lax.fori_loop(1, columns, send, 0)
+        lax.fori_loop(0, columns - 1, send, 0)
 
     def arrivals(target, which):
         rest = target.at[pl.ds(0, columns - 1)]
@@ -207,9 +255,54 @@
         rest = source.at[pl.ds(0, columns - 1)]
         pltpu.make_async_copy(rest, rest, swap_send.at[which]).wait()
 
-    exchange(packed, arrived, 0)
-    for copy in loads_in[1:]:
+    exchange(packed, arrived, 0, column_of, me_v)
+
+    uses_copy = pltpu.make_async_remote_copy(
+        src_ref=my_uses,
+        dst_ref=uses,
+        send_sem=uses_send,
+        recv_sem=uses_recv,
+        device_id=(me_c, my_owner),
+        device_id_type=MESH,
+    )
+    pl.when(moved_home)(uses_copy.start)
+
+    @pl.when(jnp.logical_not(has_low_x))
+    def _():
+        halo_x[:, :, mid:] = jnp.zeros((STEPS, 2, mid, NZ, LANES), jnp.float32)
+
+    @pl.when(jnp.logical_not(has_high_x))
+    def _():
+        halo_x[:, :, :mid] = jnp.zeros((STEPS, 2, mid, NZ, LANES), jnp.float32)
+
+    @pl.when(jnp.logical_not(has_low_y))
+    def _():
+        halo_y[:, 1] = jnp.zeros((STEPS, nvx, NZ, LANES), jnp.float32)
+
+    @pl.when(jnp.logical_not(has_high_y))
+    def _():
+        halo_y[:, 0] = jnp.zeros((STEPS, nvx, NZ, LANES), jnp.float32)
+
+    for copy in loads_in[4:]:
         copy.wait()
+    for pair in range(nvx // 2):
+        span = slice(pair * 2 * PLANE, (pair + 1) * 2 * PLANE)
+        planes[pair, :DIRS] = left[:, span]
+        planes[pair, DIRS : 2 * DIRS] = right[:, span]
+        planes[pair, 2 * DIRS : KERNELS] = loss[:, span]
+        planes[pair, KERNELS:] = jnp.zeros((NZ - KERNELS, 2 * PLANE), jnp.float32)
+    remaining = planes[...].reshape(nvx // 2 * NZ, 2 * PLANE)
+    chosen = 0.0
+    for _ in range(3):
+        top = remaining.astype(jnp.bfloat16)
+        chosen = chosen + jnp.dot(top, picks[...], preferred_element_type=jnp.float32)
+        remaining = remaining - top.astype(jnp.float32)
+    chosen = (chosen * (1.0 / (nvx * PLANE))).reshape(nvx // 2, NZ, 4 * LANES)
+    for a in range(nvx):
+        b = -a % nvx
+        near, far = a % 2 * LANES, (2 + b % 2) * LANES
+        sym[a] = chosen[a // 2, :, near : near + LANES] + chosen[b // 2, :, far : far + LANES]
+
     arrivals(arrived, 0)
 
     lane = lax.broadcasted_iota(jnp.int32, (1, 1, LANES), 2)
@@ -233,8 +326,8 @@
         routes = [
             (state.at[step, :, pl.ds(mid, mid)], halo_x.at[step, :, pl.ds(mid, mid)], (me_c + 1, me_v)),
             (state.at[step, :, pl.ds(0, mid)], halo_x.at[step, :, pl.ds(0, mid)], (me_c - 1, me_v)),
-            (state.at[step, 1], halo_y.at[step, 1], (me_c, me_v + 1)),
-            (state.at[step, 0], halo_y.at[step, 0], (me_c, me_v - 1)),
+            (state.at[step, 1], halo_y.at[step, 1], (me_c, owner_of(me_y + 1))),
+            (state.at[step, 0], halo_y.at[step, 0], (me_c, owner_of(me_y - 1))),
         ]
         return [
             pltpu.make_async_remote_copy(
@@ -289,7 +382,7 @@
         spec[1] = jnp.stack(imag)
 
         def weigh(w, carry):
-            gains = [sym[w, pl.ds(a, 1), :] for a in range(nvx)]
+            gains = [sym[a, pl.ds(w, 1), :] for a in range(nvx)]
             real, imag = fourier(
                 [spec[0, a] * gains[a] for a in range(nvx)], [spec[1, a] * gains[a] for a in range(nvx)], 1
             )
@@ -318,8 +411,8 @@
         jnp.where(lane < LOCAL_V, part[:, : NZ // 2], turn(part, LOCAL_V)[:, NZ // 2 :]) for part in parts
     ]
     packed_back[...] = jnp.stack(stacked, axis=1).reshape(columns, NZ // 2, LANES)
-    exchange(packed_back, arrived_back, 1)
-    arrived_back[pl.ds(me_v, 1)] = packed_back[pl.ds(me_v, 1)]
+    exchange(packed_back, arrived_back, 1, lambda to: to, me_y)
+    arrived_back[pl.ds(me_y, 1)] = packed_back[pl.ds(me_v, 1)]
 
     both = low + high
     sums_low, sums_high = jnp.sum(low, axis=0), jnp.sum(high, axis=0)
@@ -333,23 +426,15 @@
         (sums_low + sums_high) * lanes[8],
         squared + sums_low * lanes[9] + sums_high * lanes[10],
     ]
-    depth = lax.broadcasted_iota(jnp.int32, (NZ, LANES), 0)
-    slot = lax.broadcasted_iota(jnp.int32, (NZ, LANES), 1)
-    uses = jnp.zeros((NZ, LANES), jnp.float32)
-    per_owner = PANEL_DEV * columns
-    for n in range(WALL_SLOTS):
-        panel = wall_panel[0, 0, n]
-        target = panel // per_owner * PANEL_DEV + lax.rem(panel, PANEL_DEV)
-        target = jnp.where(n < wall_count[0, 0], target, -1)
-        hit = jnp.logical_and(depth == wall_cell[0, 0, n], slot == target)
-        uses = uses + jnp.where(hit, 1.0, 0.0)
+    pl.when(moved_home)(uses_copy.wait_recv)
+    counted = uses[...]
     shares = [
-        jnp.sum(jnp.sum(total, axis=1, keepdims=True) * uses, axis=0, keepdims=True) for total in totals
+        jnp.sum(jnp.sum(total, axis=1, keepdims=True) * counted, axis=0, keepdims=True) for total in totals
     ]
     shares.append(jnp.zeros((NZ - MOMENTS, LANES), jnp.float32))
     share = jnp.concatenate(shares, axis=0)
     mine[...] = share
-    others[pl.ds(me_c, 1)] = share[None]
+    all_others, rest = others.at[pl.ds(0, cells)], others.at[pl.ds(0, cells - 1)]
 
     def give(j, carry):
         to = lax.rem(me_c + j, cells)
@@ -358,15 +443,23 @@
             dst_ref=others.at[me_c],
             send_sem=load_send,
             recv_sem=load_recv,
-            device_id=(to, me_v),
+            device_id=(to, me_y),
             device_id_type=MESH,
         ).start()
         return carry
 
     lax.fori_loop(1, cells, give, 0)
 
-    rest = others.at[pl.ds(0, cells - 1)]
-    pltpu.make_async_copy(rest, rest, load_recv).wait()
+    @pl.when(moved_home)
+    def _():
+        give(0, 0)
+        pltpu.make_async_copy(all_others, all_others, load_recv).wait()
+
+    @pl.when(jnp.logical_not(moved_home))
+    def _():
+        others[pl.ds(me_c, 1)] = share[None]
+        pltpu.make_async_copy(rest, rest, load_recv).wait()
+
     summed = jnp.sum(others[...], axis=0)
     picked = slot - PANEL_DEV * me_c
     columns_out = [
@@ -379,11 +472,13 @@
         stop = min(start + LANES // NZ, columns)
         block = arrived_back[start:stop]
         tall = jnp.concatenate([block, turn(block, LOCAL_V)], axis=1).reshape((stop - start) * NZ, LANES)
-        out[:, start * NZ : stop * NZ] = jnp.transpose(tall)[:LOCAL_V]
+        out[:, 0, start * NZ : stop * NZ] = jnp.transpose(tall)[:LOCAL_V]
 
     departures(packed, 0)
     departures(packed_back, 1)
-    pltpu.make_async_copy(rest, rest, load_send).wait()
+    pl.when(moved_home)(uses_copy.wait_send)
+    pl.when(moved_home)(pltpu.make_async_copy(all_others, all_others, load_send).wait)
+    pl.when(jnp.logical_not(moved_home))(pltpu.make_async_copy(rest, rest, load_send).wait)
 
     def finish(step, carry):
         for copy, present in zip(halo_copies(step), sends):
@@ -393,26 +488,12 @@
     lax.fori_loop(0, STEPS, finish, 0)
 
 
-def even_weights(gain_left, gain_right, loss_kernel):
-    kernels = jnp.concatenate([gain_left, gain_right, loss_kernel[None]], axis=0)
-    full = kernels.reshape(KERNELS, -1, NVY, NVZ)
-    mirrored = full
-    for axis in (1, 2, 3):
-        mirrored = jnp.roll(jnp.flip(mirrored, axis), 1, axis)
-    count = full.shape[1] * PLANE
-    twice = np.full(KEPT, 2.0)
-    twice[0] = twice[-1] = 1.0
-    scale = jnp.asarray((0.5 * twice / count).astype(np.float32))
-    kept = (full + mirrored)[..., :KEPT] * scale
-    flat = kept.reshape(KERNELS, full.shape[1], NVY * KEPT)
-    return jnp.pad(flat, ((0, 0), (0, 0), (0, LANES - NVY * KEPT)))
-
-
 def per_device(cells, columns, distribution, gain_left, gain_right, loss_kernel, wall_cell, wall_count, wall_panel):
     nvx = columns // PARTS
     local, _, width = distribution.shape
     f32 = jnp.float32
-    sym = even_weights(gain_left, gain_right, loss_kernel)
+    loss = loss_kernel.reshape(1, -1)
+    picks = jnp.asarray(weight_selectors())
     mats = jnp.asarray(plane_matrices())
     tables = jnp.asarray(lane_tables())
     anywhere = pl.BlockSpec(memory_space=pl.ANY)
@@ -421,19 +502,22 @@
     out, loads = pl.pallas_call(
         functools.partial(kernel, cells, columns),
         out_shape=(
-            jax.ShapeDtypeStruct((local, width), f32),
+            jax.ShapeDtypeStruct((local, 1, width), f32),
             jax.ShapeDtypeStruct((MOMENTS, PANEL_DEV), f32),
         ),
-        in_specs=[anywhere] * 7,
+        in_specs=[anywhere] * 10,
         out_specs=(in_vmem, in_vmem),
         scratch_shapes=[
             pltpu.VMEM(distribution.shape, f32),
-            pltpu.VMEM(mats.shape, jnp.bfloat16),
-            pltpu.VMEM(sym.shape, f32),
-            pltpu.VMEM(tables.shape, f32),
             pltpu.SMEM(wall_cell.shape, jnp.int32),
             pltpu.SMEM(wall_count.shape, jnp.int32),
             pltpu.SMEM(wall_panel.shape, jnp.int32),
+            pltpu.VMEM(gain_left.shape, f32),
+            pltpu.VMEM(gain_right.shape, f32),
+            pltpu.VMEM(loss.shape, f32),
+            pltpu.VMEM(picks.shape, jnp.bfloat16),
+            pltpu.VMEM(mats.shape, jnp.bfloat16),
+            pltpu.VMEM(tables.shape, f32),
             pltpu.VMEM((columns, NZ // 2, LANES), f32),
             pltpu.VMEM((columns, NZ // 2, LANES), f32),
             pltpu.VMEM((columns, NZ // 2, LANES), f32),
@@ -441,25 +525,31 @@
             pltpu.VMEM((STEPS + 1, 2, nvx, NZ, LANES), f32),
             pltpu.VMEM((STEPS, 2, nvx, NZ, LANES), f32),
             pltpu.VMEM((STEPS, 2, nvx, NZ, LANES), f32),
+            pltpu.VMEM((nvx // 2, NZ, 2 * PLANE), f32),
+            pltpu.VMEM((nvx, NZ, LANES), f32),
             pltpu.VMEM((2, nvx, NZ, LANES), f32),
             pltpu.VMEM((KERNELS, nvx * NZ, 2 * LANES), f32),
             pltpu.VMEM((NZ, LANES), f32),
+            pltpu.VMEM((NZ, LANES), f32),
+            pltpu.VMEM((NZ, LANES), f32),
             pltpu.VMEM((cells, NZ, LANES), f32),
-            dma((7,)),
+            dma((10,)),
             dma((4, STEPS)),
             dma((4, STEPS)),
             dma((2,)),
             dma((2,)),
             dma,
             dma,
+            dma,
+            dma,
         ],
         compiler_params=pltpu.CompilerParams(
-            collective_id=0, has_side_effects=True, vmem_limit_bytes=32 * 1024 * 1024
+            collective_id=0, has_side_effects=True, vmem_limit_bytes=VMEM_LIMIT
         ),
         cost_estimate=pl.CostEstimate(flops=1_000_000_000, bytes_accessed=2_000_000, transcendentals=0),
         name="collide",
-    )(distribution, mats, sym, tables, wall_cell, wall_count, wall_panel)
-    return out.reshape(local, 1, width), loads
+    )(distribution, wall_cell, wall_count, wall_panel, gain_left, gain_right, loss, picks, mats, tables)
+    return out, loads
 
 
 def solution(mesh):

time: 61 us -> 56.6 us (0.928)
  the two profiles are of different devices: /device:TPU:3 before, /device:TPU:7 now
where the time goes in v1:
time: 56.6 us; the launch traced here: 56.4 us
  Pallas kernels  53 us (94%)
  local copies, waits for them, and re-layouts  2.16 us (4%)
  between operations  1.29 us (2%)
    pallas_call x1, Pallas kernels, per_device(): pl.pallas_call(functools.partial(kernel, cells, columns), out_shape=(jax....  53 us
    unnamed x4, local copies, waits for them, and re-layouts  2.16 us

profile of v1, /device:TPU:7, one launch (start us, length us, event | category | flops | bytes accessed | tf_op | source)
XLA Modules:
  0.0 56.4 jit_solution(9043737230184952337)
XLA Ops:
  1.3 53.0 %collide.1 = (f32[64,1,384]{2,1,0:T(1,128)}, f32[4,4]{1,0:T(4,128)}) custom-call(f32[64,1,384]{2,1,0:T(1,128)} %x_in.1, s32[1,1,8]{2,1,0:T(1,128)} %wall_cell_in.1, s32[1,1]{1,0:T(1,128)S(6)} %copy.14.wall_count_in, s32[1,1,8]{2,1,0:T(1,128)} %wall_panel_in.1, f32[2,3072]{1,0:T(2,128)} %left_in.1, f32[2,3072]{1,0:T(2,128)} %right_in.1, f32[1,3072]{1,0:T(1,128)} %bitcast.1, ...), custom_call_target="tpu_custom_call" | custom-call | flops 1000000000 | bytes 2000000 | tf_op jit(solution)/shard_map/collide/pallas_call | solution.py:502
  54.3 0.0 copy-start
  54.3 1.6 %copy.15 = f32[64,1,384]{2,1,0:T(1,128)} copy(f32[64,1,384]{2,1,0:T(1,128)} %get-tuple-element.4) | data formatting | bytes 196608
  55.8 0.0 copy-done
  55.9 0.6 %copy.16 = f32[4,4]{1,0:T(4,128)} copy(f32[4,4]{1,0:T(4,128)S(1)} %copy-done) | data formatting | bytes 128
Async XLA Ops:
  54.3 1.6 %copy-start = (f32[4,4]{1,0:T(4,128)S(1)}, f32[4,4]{1,0:T(4,128)}, u32[]{:S(2)}) copy-start(f32[4,4]{1,0:T(4,128)} %get-tuple-element.5) | copy-start | bytes 196

commit v2 on v1

--- a/solution.py
+++ b/solution.py
@@ -159,13 +159,22 @@
     my_owner = owner_of(me_v)
     line, place = me_v // ring, lax.rem(me_v, ring)
 
-    def descending(n, count):
-        half = (n + 1) // 2
-        return lax.rem(count // 2 + jnp.where(lax.rem(n, 2) == 1, half, -half), count)
-
-    def partner(j):
-        there = lax.rem(place + descending(j // lines, ring), ring)
-        return lax.rem(line + descending(lax.rem(j, lines), lines), lines) * ring + there
+    def for_partners(visit, start, stop):
+        def visit_round(n, shift, count):
+            there = lax.rem(place + shift, ring)
+            for m in range(count):
+                across = lines // 2 + (m + 1) // 2 * (1 if m % 2 else -1)
+                to_line = lax.rem(line + across, lines)
+                visit(to_line * ring + there, to_line * ring + lax.rem(there - 1 + to_line + ring, ring))
+
+        def one_round(n, carry):
+            half = (n + 1) // 2
+            visit_round(n, ring // 2 + jnp.where(lax.rem(n, 2) == 1, half, -half), lines)
+            return carry
+
+        lax.fori_loop(start, min(stop, ring - 1), one_round, 0)
+        if stop == ring:
+            visit_round(ring - 1, 0, lines - 1)
 
     pairs = [
         (x_in, x_v), (wall_cell_in, wall_cell), (wall_count_in, wall_count), (wall_panel_in, wall_panel),
@@ -177,9 +186,8 @@
 
     barrier = pltpu.get_barrier_semaphore()
 
-    def greet_column(j, carry):
-        pl.semaphore_signal(barrier, inc=1, device_id=(me_c, partner(j)), device_id_type=MESH)
-        return carry
+    def greet_column(to, column):
+        pl.semaphore_signal(barrier, inc=1, device_id=(me_c, to), device_id_type=MESH)
 
     def greet_row(j, carry):
         to = lax.rem(me_c + j, cells)
@@ -191,7 +199,7 @@
     moved_home = my_owner != me_v
     greetings = [(jnp.logical_and(moved_home, has_low_x), -1), (jnp.logical_and(moved_home, has_high_x), 1)]
 
-    lax.fori_loop(0, columns - 1, greet_column, 0)
+    for_partners(greet_column, 0, ring)
     lax.fori_loop(1, cells, greet_row, 0)
     greeted = columns - 1 + cells - 1
     for present, way in greetings:
@@ -232,20 +240,18 @@
 
     pl.semaphore_wait(barrier, greeted)
 
-    def exchange(source, target, which, source_slot, target_slot):
-        def send(j, carry):
-            to = partner(j)
+    def exchange(source, target, which, by_column, target_slot, start, stop):
+        def send(to, column):
             pltpu.make_async_remote_copy(
-                src_ref=source.at[source_slot(to)],
+                src_ref=source.at[column if by_column else to],
                 dst_ref=target.at[target_slot],
                 send_sem=swap_send.at[which],
                 recv_sem=swap_recv.at[which],
                 device_id=(me_c, to),
                 device_id_type=MESH,
             ).start()
-            return carry
-
-        lax.fori_loop(0, columns - 1, send, 0)
+
+        for_partners(send, start, stop)
 
     def arrivals(target, which):
         rest = target.at[pl.ds(0, columns - 1)]
@@ -255,7 +261,7 @@
         rest = source.at[pl.ds(0, columns - 1)]
         pltpu.make_async_copy(rest, rest, swap_send.at[which]).wait()
 
-    exchange(packed, arrived, 0, column_of, me_v)
+    exchange(packed, arrived, 0, True, me_v, 0, ring)
 
     uses_copy = pltpu.make_async_remote_copy(
         src_ref=my_uses,
@@ -411,8 +417,7 @@
         jnp.where(lane < LOCAL_V, part[:, : NZ // 2], turn(part, LOCAL_V)[:, NZ // 2 :]) for part in parts
     ]
     packed_back[...] = jnp.stack(stacked, axis=1).reshape(columns, NZ // 2, LANES)
-    exchange(packed_back, arrived_back, 1, lambda to: to, me_y)
-    arrived_back[pl.ds(me_y, 1)] = packed_back[pl.ds(me_v, 1)]
+    exchange(packed_back, arrived_back, 1, False, me_y, 0, ring // 2)
 
     both = low + high
     sums_low, sums_high = jnp.sum(low, axis=0), jnp.sum(high, axis=0)
@@ -449,10 +454,13 @@
         return carry
 
     lax.fori_loop(1, cells, give, 0)
+    pl.when(moved_home)(lambda: give(0, None))
+
+    exchange(packed_back, arrived_back, 1, False, me_y, ring // 2, ring)
+    arrived_back[pl.ds(me_y, 1)] = packed_back[pl.ds(me_v, 1)]
 
     @pl.when(moved_home)
     def _():
-        give(0, 0)
         pltpu.make_async_copy(all_others, all_others, load_recv).wait()
 
     @pl.when(jnp.logical_not(moved_home))
@@ -502,8 +510,8 @@
     out, loads = pl.pallas_call(
         functools.partial(kernel, cells, columns),
         out_shape=(
-            jax.ShapeDtypeStruct((local, 1, width), f32),
-            jax.ShapeDtypeStruct((MOMENTS, PANEL_DEV), f32),
+            pltpu.VMEM((local, 1, width), f32),
+            pltpu.VMEM((MOMENTS, PANEL_DEV), f32),
         ),
         in_specs=[anywhere] * 10,
         out_specs=(in_vmem, in_vmem),

time: 56.6 us -> 53.8 us (0.951)
  the two profiles are of different devices: /device:TPU:7 before, /device:TPU:1 now
where the time goes in v2:
time: 53.8 us; the launch traced here: 53.1 us
  Pallas kernels  50.6 us (94%)
  between operations  1.29 us (2%)
  local copies, waits for them, and re-layouts  1.22 us (2%)
    pallas_call x1, Pallas kernels, per_device(): pl.pallas_call(functools.partial(kernel, cells, columns), out_shape=(pltp...  50.6 us
    unnamed x2, local copies, waits for them, and re-layouts  1.22 us

profile of v2, /device:TPU:1, one launch (start us, length us, event | category | flops | bytes accessed | tf_op | source)
XLA Modules:
  0.0 53.1 jit_solution(11723367054135733466)
XLA Ops:
  1.3 50.6 %collide.1 = (f32[64,1,384]{2,1,0:T(1,128)S(1)}, f32[4,4]{1,0:T(4,128)S(1)}) custom-call(f32[64,1,384]{2,1,0:T(1,128)} %x_in.1, s32[1,1,8]{2,1,0:T(1,128)} %wall_cell_in.1, s32[1,1]{1,0:T(1,128)S(6)} %copy.16.wall_count_in, s32[1,1,8]{2,1,0:T(1,128)} %wall_panel_in.1, f32[2,3072]{1,0:T(2,128)} %left_in.1, f32[2,3072]{1,0:T(2,128)} %right_in.1, ...), custom_call_target="tpu_custom_call" | custom-call | flops 1000000000 | bytes 2000000 | tf_op jit(solution)/shard_map/collide/pallas_call | solution.py:510
  51.9 0.6 %copy.14 = f32[64,1,384]{2,1,0:T(1,128)} copy(f32[64,1,384]{2,1,0:T(1,128)S(1)} %get-tuple-element.2) | data formatting | bytes 196608
  52.5 0.6 %copy.15 = f32[4,4]{1,0:T(4,128)} copy(f32[4,4]{1,0:T(4,128)S(1)} %get-tuple-element.3) | data formatting | bytes 128

commit v3 on v2

--- a/solution.py
+++ b/solution.py
@@ -88,6 +88,24 @@
     rows.append(cube * (vy[0] ** 2 + vz**2) + 0.0 * z)
     rows.append(cube * (vy[1] ** 2 + vz**2) + 0.0 * z)
     return np.stack(rows).astype(np.float32)
+
+
+def row_tables():
+    lane = np.arange(LANES)
+    z = (np.arange(NZ)[:, None] + lane // LOCAL_V * (NZ // 2)) % NZ
+    parts = []
+    for part in range(PARTS):
+        point = part * LOCAL_V + lane % LOCAL_V
+        vy = (2 * (point // NVZ) - (NVY - 1)) * 0.5 * SPACING
+        vz = (2 * (point % NVZ) - (NVZ - 1)) * 0.5 * SPACING
+        parts.append([
+            1.0 - COURANT * (np.abs(vy) + np.abs(vz)) + 0.0 * z,
+            COURANT * np.maximum(vy, 0.0) + 0.0 * z,
+            COURANT * np.maximum(-vy, 0.0) + 0.0 * z,
+            COURANT * np.maximum(vz, 0.0) * (z > 0),
+            COURANT * np.maximum(-vz, 0.0) * (z < NZ - 1),
+        ])
+    return np.array(parts).astype(np.float32)
 
 
 def fourier(real, imag, sign):
@@ -132,12 +150,12 @@
 
 def kernel(
     cells, columns,
-    x_in, wall_cell_in, wall_count_in, wall_panel_in, left_in, right_in, loss_in, picks_in, mats_in, lanes_in,
+    x_in, wall_cell_in, wall_count_in, wall_panel_in, left_in, right_in, loss_in, picks_in, mats_in, lanes_in, own_in,
     out, loads,
-    x_v, wall_cell, wall_count, wall_panel, left, right, loss, picks, mats, lanes,
-    packed, arrived, packed_back, arrived_back, state, halo_x, halo_y,
+    x_v, wall_cell, wall_count, wall_panel, left, right, loss, picks, mats, lanes, own_rows,
+    field, packed, packed_on, arrived, arrived_on, moved, packed_back, arrived_back, state, halo_x, halo_y,
     planes, sym, spec, back, my_uses, uses, mine, others,
-    in_sems, halo_send, halo_recv, swap_send, swap_recv, load_send, load_recv, uses_send, uses_recv,
+    in_sems, halo_send, halo_recv, swap_send, swap_recv, on_send, on_recv, load_send, load_recv, uses_send, uses_recv,
 ):
     nvx = columns // PARTS
     mid = nvx // 2
@@ -155,6 +173,10 @@
         line, place = device // ring, lax.rem(device, ring)
         return line * ring + lax.rem(place - 1 + line + ring, ring)
 
+    half = columns // 2
+    goes_up = me_v >= half
+    next_c = me_c + jnp.where(goes_up, 1, -1)
+    has_next = jnp.logical_and(next_c >= 0, next_c < cells)
     me_y = column_of(me_v)
     my_owner = owner_of(me_v)
     line, place = me_v // ring, lax.rem(me_v, ring)
@@ -168,8 +190,8 @@
                 visit(to_line * ring + there, to_line * ring + lax.rem(there - 1 + to_line + ring, ring))
 
         def one_round(n, carry):
-            half = (n + 1) // 2
-            visit_round(n, ring // 2 + jnp.where(lax.rem(n, 2) == 1, half, -half), lines)
+            away = (n + 1) // 2
+            visit_round(n, ring // 2 + jnp.where(lax.rem(n, 2) == 1, away, -away), lines)
             return carry
 
         lax.fori_loop(start, min(stop, ring - 1), one_round, 0)
@@ -178,7 +200,7 @@
 
     pairs = [
         (x_in, x_v), (wall_cell_in, wall_cell), (wall_count_in, wall_count), (wall_panel_in, wall_panel),
-        (left_in, left), (right_in, right), (loss_in, loss), (picks_in, picks), (mats_in, mats), (lanes_in, lanes),
+        (left_in, left), (right_in, right), (loss_in, loss), (picks_in, picks), (mats_in, mats), (lanes_in, lanes), (own_in, own_rows),
     ]
     loads_in = [pltpu.make_async_copy(src, dst, in_sems.at[n]) for n, (src, dst) in enumerate(pairs)]
     for copy in loads_in:
@@ -188,6 +210,16 @@
 
     def greet_column(to, column):
         pl.semaphore_signal(barrier, inc=1, device_id=(me_c, to), device_id_type=MESH)
+        greet_sender(to)
+
+    def greet_sender(to):
+        upward = to >= half
+        present = jnp.logical_or(jnp.logical_and(upward, has_low_x), jnp.logical_and(to < half, has_high_x))
+
+        @pl.when(present)
+        def _():
+            neighbour = me_c + jnp.where(upward, -1, 1)
+            pl.semaphore_signal(barrier, inc=1, device_id=(neighbour, to), device_id_type=MESH)
 
     def greet_row(j, carry):
         to = lax.rem(me_c + j, cells)
@@ -200,8 +232,9 @@
     greetings = [(jnp.logical_and(moved_home, has_low_x), -1), (jnp.logical_and(moved_home, has_high_x), 1)]
 
     for_partners(greet_column, 0, ring)
+    greet_sender(me_v)
     lax.fori_loop(1, cells, greet_row, 0)
-    greeted = columns - 1 + cells - 1
+    greeted = columns - 1 + cells - 1 + jnp.where(has_next, columns, 0)
     for present, way in greetings:
         greeted = greeted + jnp.where(present, 1, 0)
 
@@ -214,11 +247,38 @@
     for start in range(0, width, LANES):
         stop = min(start + LANES, width)
         tile = x_v[:, 0, start:stop]
-        shifted = jnp.concatenate([tile[:, NZ // 2 :], tile[:, : NZ // 2]], axis=1)
+        back_by_half = jnp.concatenate([tile[:, NZ // 2 :], tile[:, : NZ // 2]], axis=1)
+        on_by_half = jnp.concatenate([tile[:, -(NZ // 2) :], tile[:, : -(NZ // 2)]], axis=1)
+        place_z = lax.rem(lax.broadcasted_iota(jnp.int32, tile.shape, 1), NZ)
+        shifted = jnp.where(place_z < NZ // 2, back_by_half, on_by_half)
         turned = jnp.transpose(jnp.concatenate([tile, shifted], axis=0))
         turned = turned.reshape((stop - start) // NZ, NZ, LANES)
-        packed[start // NZ : stop // NZ] = turned[:, : NZ // 2]
+        field[1 + start // NZ : 1 + stop // NZ] = turned
+    field[0] = jnp.zeros((NZ, LANES), jnp.float32)
+    field[columns + 1] = jnp.zeros((NZ, LANES), jnp.float32)
+
+    loads_in[10].wait()
+    part = lax.rem(me_v, PARTS)
+    weight_x = COURANT * 0.5 * SPACING * jnp.abs(2 * (me_v // PARTS) - (nvx - 1)).astype(jnp.float32)
+    here = field[1 : columns + 1]
+    stays = (
+        here * (own_rows[part, 0] - weight_x)
+        + field[:columns] * own_rows[part, 1]
+        + field[2:] * own_rows[part, 2]
+        + pltpu.roll(here, 1, 1) * own_rows[part, 3]
+        + pltpu.roll(here, NZ - 1, 1) * own_rows[part, 4]
+    )
+    packed[...] = stays[:, : NZ // 2]
+    packed_on[...] = here[:, : NZ // 2] * weight_x
     arrived[pl.ds(me_v, 1)] = packed[pl.ds(me_y, 1)]
+
+    @pl.when(jnp.logical_not(has_low_x))
+    def _():
+        arrived_on[half:] = jnp.zeros((half, NZ // 2, LANES), jnp.float32)
+
+    @pl.when(jnp.logical_not(has_high_x))
+    def _():
+        arrived_on[:half] = jnp.zeros((half, NZ // 2, LANES), jnp.float32)
 
     depth = lax.broadcasted_iota(jnp.int32, (NZ, LANES), 0)
     slot = lax.broadcasted_iota(jnp.int32, (NZ, LANES), 1)
@@ -240,18 +300,15 @@
 
     pl.semaphore_wait(barrier, greeted)
 
-    def exchange(source, target, which, by_column, target_slot, start, stop):
-        def send(to, column):
-            pltpu.make_async_remote_copy(
-                src_ref=source.at[column if by_column else to],
-                dst_ref=target.at[target_slot],
-                send_sem=swap_send.at[which],
-                recv_sem=swap_recv.at[which],
-                device_id=(me_c, to),
-                device_id_type=MESH,
-            ).start()
-
-        for_partners(send, start, stop)
+    def send_block(source, target, which, to, source_slot, target_slot):
+        pltpu.make_async_remote_copy(
+            src_ref=source.at[source_slot],
+            dst_ref=target.at[target_slot],
+            send_sem=swap_send.at[which],
+            recv_sem=swap_recv.at[which],
+            device_id=(me_c, to),
+            device_id_type=MESH,
+        ).start()
 
     def arrivals(target, which):
         rest = target.at[pl.ds(0, columns - 1)]
@@ -261,7 +318,22 @@
         rest = source.at[pl.ds(0, columns - 1)]
         pltpu.make_async_copy(rest, rest, swap_send.at[which]).wait()
 
-    exchange(packed, arrived, 0, True, me_v, 0, ring)
+    def send_on(to, column):
+        pltpu.make_async_remote_copy(
+            src_ref=packed_on.at[column],
+            dst_ref=arrived_on.at[me_v],
+            send_sem=on_send,
+            recv_sem=on_recv.at[jnp.where(goes_up, 0, 1)],
+            device_id=(next_c, to),
+            device_id_type=MESH,
+        ).start()
+
+    def send_both(to, column):
+        send_block(packed, arrived, 0, to, column, me_v)
+        pl.when(has_next)(lambda: send_on(to, column))
+
+    for_partners(send_both, 0, ring)
+    pl.when(has_next)(lambda: send_on(me_v, me_y))
 
     uses_copy = pltpu.make_async_remote_copy(
         src_ref=my_uses,
@@ -275,21 +347,21 @@
 
     @pl.when(jnp.logical_not(has_low_x))
     def _():
-        halo_x[:, :, mid:] = jnp.zeros((STEPS, 2, mid, NZ, LANES), jnp.float32)
+        halo_x[:, :, mid:] = jnp.zeros((STEPS - 1, 2, mid, NZ, LANES), jnp.float32)
 
     @pl.when(jnp.logical_not(has_high_x))
     def _():
-        halo_x[:, :, :mid] = jnp.zeros((STEPS, 2, mid, NZ, LANES), jnp.float32)
+        halo_x[:, :, :mid] = jnp.zeros((STEPS - 1, 2, mid, NZ, LANES), jnp.float32)
 
     @pl.when(jnp.logical_not(has_low_y))
     def _():
-        halo_y[:, 1] = jnp.zeros((STEPS, nvx, NZ, LANES), jnp.float32)
+        halo_y[:, 1] = jnp.zeros((STEPS - 1, nvx, NZ, LANES), jnp.float32)
 
     @pl.when(jnp.logical_not(has_high_y))
     def _():
-        halo_y[:, 0] = jnp.zeros((STEPS, nvx, NZ, LANES), jnp.float32)
-
-    for copy in loads_in[4:]:
+        halo_y[:, 0] = jnp.zeros((STEPS - 1, nvx, NZ, LANES), jnp.float32)
+
+    for copy in loads_in[4:10]:
         copy.wait()
     for pair in range(nvx // 2):
         span = slice(pair * 2 * PLANE, (pair + 1) * 2 * PLANE)
@@ -310,6 +382,9 @@
         sym[a] = chosen[a // 2, :, near : near + LANES] + chosen[b // 2, :, far : far + LANES]
 
     arrivals(arrived, 0)
+    from_low, from_high = arrived_on.at[pl.ds(half, half)], arrived_on.at[pl.ds(0, half)]
+    pl.when(has_low_x)(pltpu.make_async_copy(from_low, from_low, on_recv.at[0]).wait)
+    pl.when(has_high_x)(pltpu.make_async_copy(from_high, from_high, on_recv.at[1]).wait)
 
     lane = lax.broadcasted_iota(jnp.int32, (1, 1, LANES), 2)
     used = lane < HALF
@@ -318,13 +393,13 @@
     def turn(values, by):
         return pltpu.roll(values, by, values.ndim - 1)
 
-    blocks = arrived[...].reshape(nvx, PARTS, NZ // 2, LANES)
+    blocks = (arrived[...] + arrived_on[...]).reshape(nvx, PARTS, NZ // 2, LANES)
     wide = []
     for part in range(PARTS):
         block = blocks[:, part]
         wide.append(jnp.concatenate([block, turn(block, LOCAL_V)], axis=1))
-    state[0, 0] = jnp.where(lane < LOCAL_V, wide[0], jnp.where(used, turn(wide[1], LOCAL_V), 0.0))
-    state[0, 1] = jnp.where(
+    moved[0] = jnp.where(lane < LOCAL_V, wide[0], jnp.where(used, turn(wide[1], LOCAL_V), 0.0))
+    moved[1] = jnp.where(
         lane < quarter, turn(wide[1], LANES - quarter), jnp.where(used, turn(wide[2], quarter), 0.0)
     )
 
@@ -353,7 +428,7 @@
     def speed_x(a):
         return (2 * a - (nvx - 1)) * 0.5 * SPACING
 
-    def advance(step, carry):
+    def transport(step):
         copies = halo_copies(step)
         for copy, present in zip(copies, sends):
             pl.when(present)(copy.start)
@@ -370,14 +445,15 @@
         for copy, present in zip(copies, receives):
             pl.when(present)(copy.wait_recv)
 
-        moved = []
         for h in (0, 1):
             side = []
             for a in range(nvx):
                 weight = COURANT * abs(speed_x(a))
                 side.append(own[h][a] + (halo_x[step, h, a] - state[step, h, a]) * weight)
-            moved.append(jnp.stack(side) + halo_y[step, h] * lanes[2 + h])
-        rows = jnp.concatenate([side.reshape(nvx * NZ, LANES) for side in moved], axis=1)
+            moved[h] = jnp.stack(side) + halo_y[step, h] * lanes[2 + h]
+
+    def advance(step, carry):
+        rows = jnp.concatenate([moved[h].reshape(nvx * NZ, LANES) for h in (0, 1)], axis=1)
 
         span = 2 * LANES
         plane = exact_dot(rows, mats[:span], mats[span : 2 * span]).reshape(nvx, NZ, span)
@@ -402,12 +478,13 @@
         change = back[0] * back[2] + back[1] * back[3] - rows * back[4]
         after = rows + COLLISION_STEP * change
         for h in (0, 1):
-            state[step + 1, h] = after[:, h * LANES : (h + 1) * LANES].reshape(nvx, NZ, LANES)
+            state[step, h] = after[:, h * LANES : (h + 1) * LANES].reshape(nvx, NZ, LANES)
+        pl.when(step < STEPS - 1)(lambda: transport(step))
         return carry
 
     lax.fori_loop(0, STEPS, advance, 0)
 
-    low, high = state[STEPS, 0], state[STEPS, 1]
+    low, high = state[STEPS - 1, 0], state[STEPS - 1, 1]
     parts = [
         low,
         jnp.where(lane < quarter, turn(low, LOCAL_V), turn(high, quarter)),
@@ -417,7 +494,10 @@
         jnp.where(lane < LOCAL_V, part[:, : NZ // 2], turn(part, LOCAL_V)[:, NZ // 2 :]) for part in parts
     ]
     packed_back[...] = jnp.stack(stacked, axis=1).reshape(columns, NZ // 2, LANES)
-    exchange(packed_back, arrived_back, 1, False, me_y, 0, ring // 2)
+    def send_home(to, column):
+        send_block(packed_back, arrived_back, 1, to, to, me_y)
+
+    for_partners(send_home, 0, ring // 2)
 
     both = low + high
     sums_low, sums_high = jnp.sum(low, axis=0), jnp.sum(high, axis=0)
@@ -456,7 +536,7 @@
     lax.fori_loop(1, cells, give, 0)
     pl.when(moved_home)(lambda: give(0, None))
 
-    exchange(packed_back, arrived_back, 1, False, me_y, ring // 2, ring)
+    for_partners(send_home, ring // 2, ring)
     arrived_back[pl.ds(me_y, 1)] = packed_back[pl.ds(me_v, 1)]
 
     @pl.when(moved_home)
@@ -483,6 +563,7 @@
         out[:, 0, start * NZ : stop * NZ] = jnp.transpose(tall)[:LOCAL_V]
 
     departures(packed, 0)
+    pl.when(has_next)(pltpu.make_async_copy(packed_on, packed_on, on_send).wait)
     departures(packed_back, 1)
     pl.when(moved_home)(uses_copy.wait_send)
     pl.when(moved_home)(pltpu.make_async_copy(all_others, all_others, load_send).wait)
@@ -493,7 +574,7 @@
             pl.when(present)(copy.wait_send)
         return carry
 
-    lax.fori_loop(0, STEPS, finish, 0)
+    lax.fori_loop(0, STEPS - 1, finish, 0)
 
 
 def per_device(cells, columns, distribution, gain_left, gain_right, loss_kernel, wall_cell, wall_count, wall_panel):
@@ -504,6 +585,7 @@
     picks = jnp.asarray(weight_selectors())
     mats = jnp.asarray(plane_matrices())
     tables = jnp.asarray(lane_tables())
+    rows = jnp.asarray(row_tables())
     anywhere = pl.BlockSpec(memory_space=pl.ANY)
     in_vmem = pl.BlockSpec(memory_space=pltpu.VMEM)
     dma = pltpu.SemaphoreType.DMA
@@ -513,7 +595,7 @@
             pltpu.VMEM((local, 1, width), f32),
             pltpu.VMEM((MOMENTS, PANEL_DEV), f32),
         ),
-        in_specs=[anywhere] * 10,
+        in_specs=[anywhere] * 11,
         out_specs=(in_vmem, in_vmem),
         scratch_shapes=[
             pltpu.VMEM(distribution.shape, f32),
@@ -526,13 +608,18 @@
             pltpu.VMEM(picks.shape, jnp.bfloat16),
             pltpu.VMEM(mats.shape, jnp.bfloat16),
             pltpu.VMEM(tables.shape, f32),
+            pltpu.VMEM(rows.shape, f32),
+            pltpu.VMEM((columns + 2, NZ, LANES), f32),
             pltpu.VMEM((columns, NZ // 2, LANES), f32),
             pltpu.VMEM((columns, NZ // 2, LANES), f32),
             pltpu.VMEM((columns, NZ // 2, LANES), f32),
             pltpu.VMEM((columns, NZ // 2, LANES), f32),
-            pltpu.VMEM((STEPS + 1, 2, nvx, NZ, LANES), f32),
+            pltpu.VMEM((2, nvx, NZ, LANES), f32),
+            pltpu.VMEM((columns, NZ // 2, LANES), f32),
+            pltpu.VMEM((columns, NZ // 2, LANES), f32),
             pltpu.VMEM((STEPS, 2, nvx, NZ, LANES), f32),
-            pltpu.VMEM((STEPS, 2, nvx, NZ, LANES), f32),
+            pltpu.VMEM((STEPS - 1, 2, nvx, NZ, LANES), f32),
+            pltpu.VMEM((STEPS - 1, 2, nvx, NZ, LANES), f32),
             pltpu.VMEM((nvx // 2, NZ, 2 * PLANE), f32),
             pltpu.VMEM((nvx, NZ, LANES), f32),
             pltpu.VMEM((2, nvx, NZ, LANES), f32),
@@ -541,10 +628,12 @@
             pltpu.VMEM((NZ, LANES), f32),
             pltpu.VMEM((NZ, LANES), f32),
             pltpu.VMEM((cells, NZ, LANES), f32),
-            dma((10,)),
-            dma((4, STEPS)),
-            dma((4, STEPS)),
+            dma((11,)),
+            dma((4, STEPS - 1)),
+            dma((4, STEPS - 1)),
             dma((2,)),
+            dma((2,)),
+            dma,
             dma((2,)),
             dma,
             dma,
@@ -556,7 +645,7 @@
         ),
         cost_estimate=pl.CostEstimate(flops=1_000_000_000, bytes_accessed=2_000_000, transcendentals=0),
         name="collide",
-    )(distribution, wall_cell, wall_count, wall_panel, gain_left, gain_right, loss, picks, mats, tables)
+    )(distribution, wall_cell, wall_count, wall_panel, gain_left, gain_right, loss, picks, mats, tables, rows)
     return out, loads
 
 

time: 53.8 us -> 53.7 us (level); the launches traced: 53.1 us -> 53.5 us
  no operation moved by 1% of the time
where the time goes in v3:
time: 53.7 us; the launch traced here: 53.5 us
  Pallas kernels  51 us (95%)
  between operations  1.29 us (2%)
  local copies, waits for them, and re-layouts  1.22 us (2%)
    pallas_call x1, Pallas kernels, per_device(): pl.pallas_call(functools.partial(kernel, cells, columns), out_shape=(pltp...  51 us
    unnamed x2, local copies, waits for them, and re-layouts  1.22 us

profile of v3, /device:TPU:1, one launch (start us, length us, event | category | flops | bytes accessed | tf_op | source)
XLA Modules:
  0.0 53.5 jit_solution(13254485371810829439)
XLA Ops:
  1.3 51.0 %collide.1 = (f32[64,1,384]{2,1,0:T(1,128)S(1)}, f32[4,4]{1,0:T(4,128)S(1)}) custom-call(f32[64,1,384]{2,1,0:T(1,128)} %x_in.1, s32[1,1,8]{2,1,0:T(1,128)} %wall_cell_in.1, s32[1,1]{1,0:T(1,128)S(6)} %copy.17.wall_count_in, s32[1,1,8]{2,1,0:T(1,128)} %wall_panel_in.1, f32[2,3072]{1,0:T(2,128)} %left_in.1, f32[2,3072]{1,0:T(2,128)} %right_in.1, ...), custom_call_target="tpu_custom_call" | custom-call | flops 1000000000 | bytes 2000000 | tf_op jit(solution)/shard_map/collide/pallas_call | solution.py:592
  52.3 0.6 %copy.15 = f32[64,1,384]{2,1,0:T(1,128)} copy(f32[64,1,384]{2,1,0:T(1,128)S(1)} %get-tuple-element.2) | data formatting | bytes 196608
  53.0 0.6 %copy.16 = f32[4,4]{1,0:T(4,128)} copy(f32[4,4]{1,0:T(4,128)S(1)} %get-tuple-element.3) | data formatting | bytes 128

commit v4 on v3

--- a/solution.py
+++ b/solution.py
@@ -51,7 +51,7 @@
                 table[row, kb * KEPT + kc] = math.cos(angle)
                 table[row, LANES + kb * KEPT + kc] = -math.sin(angle)
     high, low = split(table)
-    return np.concatenate([high, low, high.T, low.T], axis=0)
+    return np.concatenate([high, high, low, high.T, high.T, low.T], axis=0)
 
 
 def weight_selectors():
@@ -141,11 +141,10 @@
     return out_r, out_i
 
 
-def exact_dot(values, high, low):
+def three_parts(values):
     top = values.astype(jnp.bfloat16)
     rest = (values - top.astype(jnp.float32)).astype(jnp.bfloat16)
-    dot = functools.partial(jnp.dot, preferred_element_type=jnp.float32)
-    return dot(top, high) + (dot(rest, high) + dot(top, low))
+    return jnp.concatenate([top, rest, top], axis=1)
 
 
 def kernel(
@@ -181,22 +180,37 @@
     my_owner = owner_of(me_v)
     line, place = me_v // ring, lax.rem(me_v, ring)
 
-    def for_partners(visit, start, stop):
-        def visit_round(n, shift, count):
-            there = lax.rem(place + shift, ring)
-            for m in range(count):
-                across = lines // 2 + (m + 1) // 2 * (1 if m % 2 else -1)
-                to_line = lax.rem(line + across, lines)
-                visit(to_line * ring + there, to_line * ring + lax.rem(there - 1 + to_line + ring, ring))
-
+    def wrapped(value, count):
+        return jnp.where(value >= count, value - count, value)
+
+    across = [lines // 2 + (m + 1) // 2 * (1 if m % 2 else -1) for m in range(lines)]
+    to_lines = [wrapped(line + shift % lines, lines) for shift in across]
+
+    def visit_line(visit, there, m):
+        column = there + to_lines[m] - 1
+        column = wrapped(jnp.where(column < 0, column + ring, column), ring)
+        visit(to_lines[m] * ring + there, to_lines[m] * ring + column)
+
+    def farthest_first(visit):
         def one_round(n, carry):
             away = (n + 1) // 2
-            visit_round(n, ring // 2 + jnp.where(lax.rem(n, 2) == 1, away, -away), lines)
+            there = wrapped(place + ring // 2 + jnp.where(lax.rem(n, 2) == 1, away, -away), ring)
+            for m in range(lines):
+                visit_line(visit, there, m)
             return carry
 
-        lax.fori_loop(start, min(stop, ring - 1), one_round, 0)
-        if stop == ring:
-            visit_round(ring - 1, 0, lines - 1)
+        lax.fori_loop(0, ring - 1, one_round, 0)
+        for m in range(lines - 1):
+            visit_line(visit, place, m)
+
+    def in_place_order(visit, start, stop):
+        def one_round(there, carry):
+            for m in range(lines - 1):
+                visit_line(visit, there, m)
+            pl.when(there != place)(lambda: visit_line(visit, there, lines - 1))
+            return carry
+
+        lax.fori_loop(start, stop, one_round, 0)
 
     pairs = [
         (x_in, x_v), (wall_cell_in, wall_cell), (wall_count_in, wall_count), (wall_panel_in, wall_panel),
@@ -231,7 +245,7 @@
     moved_home = my_owner != me_v
     greetings = [(jnp.logical_and(moved_home, has_low_x), -1), (jnp.logical_and(moved_home, has_high_x), 1)]
 
-    for_partners(greet_column, 0, ring)
+    farthest_first(greet_column)
     greet_sender(me_v)
     lax.fori_loop(1, cells, greet_row, 0)
     greeted = columns - 1 + cells - 1 + jnp.where(has_next, columns, 0)
@@ -318,22 +332,31 @@
         rest = source.at[pl.ds(0, columns - 1)]
         pltpu.make_async_copy(rest, rest, swap_send.at[which]).wait()
 
+    on_way = jnp.where(goes_up, 0, 1)
+
     def send_on(to, column):
         pltpu.make_async_remote_copy(
             src_ref=packed_on.at[column],
             dst_ref=arrived_on.at[me_v],
             send_sem=on_send,
-            recv_sem=on_recv.at[jnp.where(goes_up, 0, 1)],
+            recv_sem=on_recv.at[on_way],
             device_id=(next_c, to),
             device_id_type=MESH,
         ).start()
 
+    def send_one(to, column):
+        send_block(packed, arrived, 0, to, column, me_v)
+
     def send_both(to, column):
-        send_block(packed, arrived, 0, to, column, me_v)
-        pl.when(has_next)(lambda: send_on(to, column))
-
-    for_partners(send_both, 0, ring)
-    pl.when(has_next)(lambda: send_on(me_v, me_y))
+        send_one(to, column)
+        send_on(to, column)
+
+    @pl.when(has_next)
+    def _():
+        farthest_first(send_both)
+        send_on(me_v, me_y)
+
+    pl.when(jnp.logical_not(has_next))(lambda: farthest_first(send_one))
 
     uses_copy = pltpu.make_async_remote_copy(
         src_ref=my_uses,
@@ -456,7 +479,8 @@
         rows = jnp.concatenate([moved[h].reshape(nvx * NZ, LANES) for h in (0, 1)], axis=1)
 
         span = 2 * LANES
-        plane = exact_dot(rows, mats[:span], mats[span : 2 * span]).reshape(nvx, NZ, span)
+        plane = jnp.dot(three_parts(rows), mats[: 3 * span], preferred_element_type=jnp.float32)
+        plane = plane.reshape(nvx, NZ, span)
         real, imag = fourier(
             [plane[a, :, :LANES] for a in range(nvx)], [plane[a, :, LANES:] for a in range(nvx)], -1
         )
@@ -471,11 +495,14 @@
             line = jnp.concatenate(
                 [jnp.concatenate(real, axis=0), jnp.concatenate(imag, axis=0)], axis=1
             )
-            back[w] = exact_dot(line, mats[2 * span : 3 * span], mats[3 * span :])
+            tall = nvx * NZ
+            back[pl.ds(pl.multiple_of(w * tall, tall), tall)] = three_parts(line)
             return carry
 
         lax.fori_loop(0, KERNELS, weigh, 0, unroll=True)
-        change = back[0] * back[2] + back[1] * back[3] - rows * back[4]
+        found = jnp.dot(back[...], mats[3 * span :], preferred_element_type=jnp.float32)
+        found = found.reshape(KERNELS, nvx * NZ, span)
+        change = found[0] * found[2] + found[1] * found[3] - rows * found[4]
         after = rows + COLLISION_STEP * change
         for h in (0, 1):
             state[step, h] = after[:, h * LANES : (h + 1) * LANES].reshape(nvx, NZ, LANES)
@@ -497,7 +524,7 @@
     def send_home(to, column):
         send_block(packed_back, arrived_back, 1, to, to, me_y)
 
-    for_partners(send_home, 0, ring // 2)
+    in_place_order(send_home, 0, ring // 4)
 
     both = low + high
     sums_low, sums_high = jnp.sum(low, axis=0), jnp.sum(high, axis=0)
@@ -536,7 +563,7 @@
     lax.fori_loop(1, cells, give, 0)
     pl.when(moved_home)(lambda: give(0, None))
 
-    for_partners(send_home, ring // 2, ring)
+    in_place_order(send_home, ring // 4, ring)
     arrived_back[pl.ds(me_y, 1)] = packed_back[pl.ds(me_v, 1)]
 
     @pl.when(moved_home)
@@ -623,7 +650,7 @@
             pltpu.VMEM((nvx // 2, NZ, 2 * PLANE), f32),
             pltpu.VMEM((nvx, NZ, LANES), f32),
             pltpu.VMEM((2, nvx, NZ, LANES), f32),
-            pltpu.VMEM((KERNELS, nvx * NZ, 2 * LANES), f32),
+            pltpu.VMEM((KERNELS * nvx * NZ, 6 * LANES), jnp.bfloat16),
             pltpu.VMEM((NZ, LANES), f32),
             pltpu.VMEM((NZ, LANES), f32),
             pltpu.VMEM((NZ, LANES), f32),

time: 53.7 us -> 52 us (0.968)
  Pallas kernels: 51 us -> 49.3 us
    pallas_call x1, Pallas kernels: 51 us -> 49.3 us  [per_device(): pl.pallas_call(functools.partial(kernel, cells, columns), out_shape=(pltp...]
where the time goes in v4:
time: 52 us; the launch traced here: 51.8 us
  Pallas kernels  49.3 us (95%)
  between operations  1.29 us (2%)
  local copies, waits for them, and re-layouts  1.22 us (2%)
    pallas_call x1, Pallas kernels, per_device(): pl.pallas_call(functools.partial(kernel, cells, columns), out_shape=(pltp...  49.3 us
    unnamed x2, local copies, waits for them, and re-layouts  1.22 us

profile of v4, /device:TPU:1, one launch (start us, length us, event | category | flops | bytes accessed | tf_op | source)
XLA Modules:
  0.0 51.8 jit_solution(10568431108355683411)
XLA Ops:
  1.3 49.3 %collide.1 = (f32[64,1,384]{2,1,0:T(1,128)S(1)}, f32[4,4]{1,0:T(4,128)S(1)}) custom-call(f32[64,1,384]{2,1,0:T(1,128)} %x_in.1, s32[1,1,8]{2,1,0:T(1,128)} %wall_cell_in.1, s32[1,1]{1,0:T(1,128)S(6)} %copy.17.wall_count_in, s32[1,1,8]{2,1,0:T(1,128)} %wall_panel_in.1, f32[2,3072]{1,0:T(2,128)} %left_in.1, f32[2,3072]{1,0:T(2,128)} %right_in.1, ...), custom_call_target="tpu_custom_call" | custom-call | flops 1000000000 | bytes 2000000 | tf_op jit(solution)/shard_map/collide/pallas_call | solution.py:619
  50.6 0.6 %copy.15 = f32[64,1,384]{2,1,0:T(1,128)} copy(f32[64,1,384]{2,1,0:T(1,128)S(1)} %get-tuple-element.2) | data formatting | bytes 196608
  51.2 0.6 %copy.16 = f32[4,4]{1,0:T(4,128)} copy(f32[4,4]{1,0:T(4,128)S(1)} %get-tuple-element.3) | data formatting | bytes 128

commit v5 on v4

--- a/solution.py
+++ b/solution.py
@@ -191,7 +191,7 @@
         column = wrapped(jnp.where(column < 0, column + ring, column), ring)
         visit(to_lines[m] * ring + there, to_lines[m] * ring + column)
 
-    def farthest_first(visit):
+    def farthest_first(visit, start, stop):
         def one_round(n, carry):
             away = (n + 1) // 2
             there = wrapped(place + ring // 2 + jnp.where(lax.rem(n, 2) == 1, away, -away), ring)
@@ -199,9 +199,10 @@
                 visit_line(visit, there, m)
             return carry
 
-        lax.fori_loop(0, ring - 1, one_round, 0)
-        for m in range(lines - 1):
-            visit_line(visit, place, m)
+        lax.fori_loop(start, min(stop, ring - 1), one_round, 0)
+        if stop == ring:
+            for m in range(lines - 1):
+                visit_line(visit, place, m)
 
     def in_place_order(visit, start, stop):
         def one_round(there, carry):
@@ -217,8 +218,7 @@
         (left_in, left), (right_in, right), (loss_in, loss), (picks_in, picks), (mats_in, mats), (lanes_in, lanes), (own_in, own_rows),
     ]
     loads_in = [pltpu.make_async_copy(src, dst, in_sems.at[n]) for n, (src, dst) in enumerate(pairs)]
-    for copy in loads_in:
-        copy.start()
+    loads_in[0].start()
 
     barrier = pltpu.get_barrier_semaphore()
 
@@ -245,9 +245,10 @@
     moved_home = my_owner != me_v
     greetings = [(jnp.logical_and(moved_home, has_low_x), -1), (jnp.logical_and(moved_home, has_high_x), 1)]
 
-    farthest_first(greet_column)
+    farthest_first(greet_column, 0, ring // 4)
+    lax.fori_loop(1, cells, greet_row, 0)
+    farthest_first(greet_column, ring // 4, ring)
     greet_sender(me_v)
-    lax.fori_loop(1, cells, greet_row, 0)
     greeted = columns - 1 + cells - 1 + jnp.where(has_next, columns, 0)
     for present, way in greetings:
         greeted = greeted + jnp.where(present, 1, 0)
@@ -255,6 +256,9 @@
         @pl.when(present)
         def _():
             pl.semaphore_signal(barrier, inc=1, device_id=(me_c + way, me_v), device_id_type=MESH)
+
+    for copy in loads_in[1:]:
+        copy.start()
 
     loads_in[0].wait()
     width = NZ * columns
@@ -353,10 +357,10 @@
 
     @pl.when(has_next)
     def _():
-        farthest_first(send_both)
+        farthest_first(send_both, 0, ring)
         send_on(me_v, me_y)
 
-    pl.when(jnp.logical_not(has_next))(lambda: farthest_first(send_one))
+    pl.when(jnp.logical_not(has_next))(lambda: farthest_first(send_one, 0, ring))
 
     uses_copy = pltpu.make_async_remote_copy(
         src_ref=my_uses,
@@ -428,10 +432,10 @@
 
     def halo_copies(step):
         routes = [
+            (state.at[step, 1], halo_y.at[step, 1], (me_c, owner_of(me_y + 1))),
+            (state.at[step, 0], halo_y.at[step, 0], (me_c, owner_of(me_y - 1))),
             (state.at[step, :, pl.ds(mid, mid)], halo_x.at[step, :, pl.ds(mid, mid)], (me_c + 1, me_v)),
             (state.at[step, :, pl.ds(0, mid)], halo_x.at[step, :, pl.ds(0, mid)], (me_c - 1, me_v)),
-            (state.at[step, 1], halo_y.at[step, 1], (me_c, owner_of(me_y + 1))),
-            (state.at[step, 0], halo_y.at[step, 0], (me_c, owner_of(me_y - 1))),
         ]
         return [
             pltpu.make_async_remote_copy(
@@ -445,8 +449,8 @@
             for n, (src, dst, to) in enumerate(routes)
         ]
 
-    sends = [has_high_x, has_low_x, has_high_y, has_low_y]
-    receives = [has_low_x, has_high_x, has_low_y, has_high_y]
+    sends = [has_high_y, has_low_y, has_high_x, has_low_x]
+    receives = [has_low_y, has_high_y, has_low_x, has_high_x]
 
     def speed_x(a):
         return (2 * a - (nvx - 1)) * 0.5 * SPACING

time: 52 us -> 52.1 us (level)
  no operation moved by 1% of the time
where the time goes in v5:
time: 52.1 us; the launch traced here: 51.9 us
  Pallas kernels  49.4 us (95%)
  between operations  1.29 us (2%)
  local copies, waits for them, and re-layouts  1.22 us (2%)
    pallas_call x1, Pallas kernels, per_device(): pl.pallas_call(functools.partial(kernel, cells, columns), out_shape=(pltp...  49.4 us
    unnamed x2, local copies, waits for them, and re-layouts  1.22 us

profile of v5, /device:TPU:1, one launch (start us, length us, event | category | flops | bytes accessed | tf_op | source)
XLA Modules:
  0.0 51.9 jit_solution(9573217371922371893)
XLA Ops:
  1.3 49.4 %collide.1 = (f32[64,1,384]{2,1,0:T(1,128)S(1)}, f32[4,4]{1,0:T(4,128)S(1)}) custom-call(f32[64,1,384]{2,1,0:T(1,128)} %x_in.1, s32[1,1,8]{2,1,0:T(1,128)} %wall_cell_in.1, s32[1,1]{1,0:T(1,128)S(6)} %copy.17.wall_count_in, s32[1,1,8]{2,1,0:T(1,128)} %wall_panel_in.1, f32[2,3072]{1,0:T(2,128)} %left_in.1, f32[2,3072]{1,0:T(2,128)} %right_in.1, ...), custom_call_target="tpu_custom_call" | custom-call | flops 1000000000 | bytes 2000000 | tf_op jit(solution)/shard_map/collide/pallas_call | solution.py:623
  50.7 0.6 %copy.15 = f32[64,1,384]{2,1,0:T(1,128)} copy(f32[64,1,384]{2,1,0:T(1,128)S(1)} %get-tuple-element.2) | data formatting | bytes 196608
  51.4 0.6 %copy.16 = f32[4,4]{1,0:T(4,128)} copy(f32[4,4]{1,0:T(4,128)S(1)} %get-tuple-element.3) | data formatting | bytes 128

commit v6 on v5

--- a/solution.py
+++ b/solution.py
@@ -152,9 +152,9 @@
     x_in, wall_cell_in, wall_count_in, wall_panel_in, left_in, right_in, loss_in, picks_in, mats_in, lanes_in, own_in,
     out, loads,
     x_v, wall_cell, wall_count, wall_panel, left, right, loss, picks, mats, lanes, own_rows,
-    field, packed, packed_on, arrived, arrived_on, moved, packed_back, arrived_back, state, halo_x, halo_y,
+    field, packed, packed_on, from_mate, arrived, arrived_on, moved, packed_back, arrived_back, state, halo_x, halo_y,
     planes, sym, spec, back, my_uses, uses, mine, others,
-    in_sems, halo_send, halo_recv, swap_send, swap_recv, on_send, on_recv, load_send, load_recv, uses_send, uses_recv,
+    in_sems, halo_send, halo_recv, swap_send, swap_recv, on_send, on_recv, give_send, give_recv, load_send, load_recv, uses_send, uses_recv,
 ):
     nvx = columns // PARTS
     mid = nvx // 2
@@ -176,6 +176,12 @@
     goes_up = me_v >= half
     next_c = me_c + jnp.where(goes_up, 1, -1)
     has_next = jnp.logical_and(next_c >= 0, next_c < cells)
+    even = lax.rem(me_c, 2) == 0
+    mate = me_c + jnp.where(even, 1, -1)
+    gives = next_c == mate
+    sends_on = jnp.logical_and(has_next, jnp.logical_not(gives))
+    low_sends = jnp.logical_and(even, me_c > 0)
+    high_sends = jnp.logical_and(jnp.logical_not(even), me_c < cells - 1)
     me_y = column_of(me_v)
     my_owner = owner_of(me_v)
     line, place = me_v // ring, lax.rem(me_v, ring)
@@ -228,7 +234,7 @@
 
     def greet_sender(to):
         upward = to >= half
-        present = jnp.logical_or(jnp.logical_and(upward, has_low_x), jnp.logical_and(to < half, has_high_x))
+        present = jnp.logical_or(jnp.logical_and(upward, low_sends), jnp.logical_and(to < half, high_sends))
 
         @pl.when(present)
         def _():
@@ -249,7 +255,12 @@
     lax.fori_loop(1, cells, greet_row, 0)
     farthest_first(greet_column, ring // 4, ring)
     greet_sender(me_v)
-    greeted = columns - 1 + cells - 1 + jnp.where(has_next, columns, 0)
+
+    @pl.when(jnp.logical_not(gives))
+    def _():
+        pl.semaphore_signal(barrier, inc=1, device_id=(mate, me_v), device_id_type=MESH)
+
+    greeted = columns - 1 + cells - 1 + jnp.where(gives, 1, jnp.where(sends_on, columns, 0))
     for present, way in greetings:
         greeted = greeted + jnp.where(present, 1, 0)
 
@@ -288,13 +299,12 @@
     )
     packed[...] = stays[:, : NZ // 2]
     packed_on[...] = here[:, : NZ // 2] * weight_x
-    arrived[pl.ds(me_v, 1)] = packed[pl.ds(me_y, 1)]
-
-    @pl.when(jnp.logical_not(has_low_x))
+
+    @pl.when(jnp.logical_not(low_sends))
     def _():
         arrived_on[half:] = jnp.zeros((half, NZ // 2, LANES), jnp.float32)
 
-    @pl.when(jnp.logical_not(has_high_x))
+    @pl.when(jnp.logical_not(high_sends))
     def _():
         arrived_on[:half] = jnp.zeros((half, NZ // 2, LANES), jnp.float32)
 
@@ -351,16 +361,29 @@
     def send_one(to, column):
         send_block(packed, arrived, 0, to, column, me_v)
 
-    def send_both(to, column):
-        send_one(to, column)
-        send_on(to, column)
-
-    @pl.when(has_next)
-    def _():
-        farthest_first(send_both, 0, ring)
+    give_copy = pltpu.make_async_remote_copy(
+        src_ref=packed_on,
+        dst_ref=from_mate,
+        send_sem=give_send,
+        recv_sem=give_recv,
+        device_id=(mate, me_v),
+        device_id_type=MESH,
+    )
+    pl.when(gives)(give_copy.start)
+
+    @pl.when(jnp.logical_not(gives))
+    def _():
+        pl.when(sends_on)(lambda: farthest_first(send_on, 0, ring // 4))
+        give_copy.wait_recv()
+        packed[...] = packed[...] + from_mate[...]
+
+    farthest_first(send_one, 0, ring)
+    arrived[pl.ds(me_v, 1)] = packed[pl.ds(me_y, 1)]
+
+    @pl.when(sends_on)
+    def _():
+        farthest_first(send_on, ring // 4, ring)
         send_on(me_v, me_y)
-
-    pl.when(jnp.logical_not(has_next))(lambda: farthest_first(send_one, 0, ring))
 
     uses_copy = pltpu.make_async_remote_copy(
         src_ref=my_uses,
@@ -410,8 +433,8 @@
 
     arrivals(arrived, 0)
     from_low, from_high = arrived_on.at[pl.ds(half, half)], arrived_on.at[pl.ds(0, half)]
-    pl.when(has_low_x)(pltpu.make_async_copy(from_low, from_low, on_recv.at[0]).wait)
-    pl.when(has_high_x)(pltpu.make_async_copy(from_high, from_high, on_recv.at[1]).wait)
+    pl.when(low_sends)(pltpu.make_async_copy(from_low, from_low, on_recv.at[0]).wait)
+    pl.when(high_sends)(pltpu.make_async_copy(from_high, from_high, on_recv.at[1]).wait)
 
     lane = lax.broadcasted_iota(jnp.int32, (1, 1, LANES), 2)
     used = lane < HALF
@@ -594,7 +617,8 @@
         out[:, 0, start * NZ : stop * NZ] = jnp.transpose(tall)[:LOCAL_V]
 
     departures(packed, 0)
-    pl.when(has_next)(pltpu.make_async_copy(packed_on, packed_on, on_send).wait)
+    pl.when(sends_on)(pltpu.make_async_copy(packed_on, packed_on, on_send).wait)
+    pl.when(gives)(give_copy.wait_send)
     departures(packed_back, 1)
     pl.when(moved_home)(uses_copy.wait_send)
     pl.when(moved_home)(pltpu.make_async_copy(all_others, all_others, load_send).wait)
@@ -645,6 +669,7 @@
             pltpu.VMEM((columns, NZ // 2, LANES), f32),
             pltpu.VMEM((columns, NZ // 2, LANES), f32),
             pltpu.VMEM((columns, NZ // 2, LANES), f32),
+            pltpu.VMEM((columns, NZ // 2, LANES), f32),
             pltpu.VMEM((2, nvx, NZ, LANES), f32),
             pltpu.VMEM((columns, NZ // 2, LANES), f32),
             pltpu.VMEM((columns, NZ // 2, LANES), f32),
@@ -670,6 +695,8 @@
             dma,
             dma,
             dma,
+            dma,
+            dma,
         ],
         compiler_params=pltpu.CompilerParams(
             collective_id=0, has_side_effects=True, vmem_limit_bytes=VMEM_LIMIT

time: 52.1 us -> 51.2 us (0.983)
  Pallas kernels: 49.4 us -> 48.1 us
    pallas_call x1, Pallas kernels: 49.4 us -> 48.1 us  [per_device(): pl.pallas_call(functools.partial(kernel, cells, columns), out_shape=(pltp...]
where the time goes in v6:
time: 51.2 us; the launch traced here: 50.6 us
  Pallas kernels  48.1 us (94%)
  between operations  1.29 us (3%)
  local copies, waits for them, and re-layouts  1.22 us (2%)
    pallas_call x1, Pallas kernels, per_device(): pl.pallas_call(functools.partial(kernel, cells, columns), out_shape=(pltp...  48.1 us
    unnamed x2, local copies, waits for them, and re-layouts  1.22 us

profile of v6, /device:TPU:1, one launch (start us, length us, event | category | flops | bytes accessed | tf_op | source)
XLA Modules:
  0.0 50.6 jit_solution(4553542930939290032)
XLA Ops:
  1.3 48.1 %collide.1 = (f32[64,1,384]{2,1,0:T(1,128)S(1)}, f32[4,4]{1,0:T(4,128)S(1)}) custom-call(f32[64,1,384]{2,1,0:T(1,128)} %x_in.1, s32[1,1,8]{2,1,0:T(1,128)} %wall_cell_in.1, s32[1,1]{1,0:T(1,128)S(6)} %copy.17.wall_count_in, s32[1,1,8]{2,1,0:T(1,128)} %wall_panel_in.1, f32[2,3072]{1,0:T(2,128)} %left_in.1, f32[2,3072]{1,0:T(2,128)} %right_in.1, ...), custom_call_target="tpu_custom_call" | custom-call | flops 1000000000 | bytes 2000000 | tf_op jit(solution)/shard_map/collide/pallas_call | solution.py:647
  49.4 0.6 %copy.15 = f32[64,1,384]{2,1,0:T(1,128)} copy(f32[64,1,384]{2,1,0:T(1,128)S(1)} %get-tuple-element.2) | data formatting | bytes 196608
  50.0 0.6 %copy.16 = f32[4,4]{1,0:T(4,128)} copy(f32[4,4]{1,0:T(4,128)S(1)} %get-tuple-element.3) | data formatting | bytes 128

commit v7 on v6

--- a/solution.py
+++ b/solution.py
@@ -163,14 +163,15 @@
 
     lines = 4 if columns % 4 == 0 else 2
     ring = columns // lines
+    lead = lines - 1
 
     def owner_of(column):
         line, place = column // ring, lax.rem(column, ring)
-        return line * ring + lax.rem(place + 1 - line + ring, ring)
+        return line * ring + lax.rem(place + lead - line + ring, ring)
 
     def column_of(device):
         line, place = device // ring, lax.rem(device, ring)
-        return line * ring + lax.rem(place - 1 + line + ring, ring)
+        return line * ring + lax.rem(place - lead + line + ring, ring)
 
     half = columns // 2
     goes_up = me_v >= half
@@ -193,7 +194,7 @@
     to_lines = [wrapped(line + shift % lines, lines) for shift in across]
 
     def visit_line(visit, there, m):
-        column = there + to_lines[m] - 1
+        column = there + to_lines[m] - lead
         column = wrapped(jnp.where(column < 0, column + ring, column), ring)
         visit(to_lines[m] * ring + there, to_lines[m] * ring + column)
 
@@ -551,7 +552,7 @@
     def send_home(to, column):
         send_block(packed_back, arrived_back, 1, to, to, me_y)
 
-    in_place_order(send_home, 0, ring // 4)
+    in_place_order(send_home, 0, ring // 6)
 
     both = low + high
     sums_low, sums_high = jnp.sum(low, axis=0), jnp.sum(high, axis=0)
@@ -590,7 +591,7 @@
     lax.fori_loop(1, cells, give, 0)
     pl.when(moved_home)(lambda: give(0, None))
 
-    in_place_order(send_home, ring // 4, ring)
+    in_place_order(send_home, ring // 6, ring)
     arrived_back[pl.ds(me_y, 1)] = packed_back[pl.ds(me_v, 1)]
 
     @pl.when(moved_home)

time: 51.2 us -> 53.7 us (1.049)
  Pallas kernels: 48.1 us -> 51 us
    pallas_call x1, Pallas kernels: 48.1 us -> 51 us  [per_device(): pl.pallas_call(functools.partial(kernel, cells, columns), out_shape=(pltp...]
where the time goes in v7:
time: 53.7 us; the launch traced here: 53.5 us
  Pallas kernels  51 us (95%)
  between operations  1.29 us (2%)
  local copies, waits for them, and re-layouts  1.22 us (2%)
    pallas_call x1, Pallas kernels, per_device(): pl.pallas_call(functools.partial(kernel, cells, columns), out_shape=(pltp...  51 us
    unnamed x2, local copies, waits for them, and re-layouts  1.22 us

profile of v7, /device:TPU:1, one launch (start us, length us, event | category | flops | bytes accessed | tf_op | source)
XLA Modules:
  0.0 53.5 jit_solution(13513486082586589760)
XLA Ops:
  1.3 51.0 %collide.1 = (f32[64,1,384]{2,1,0:T(1,128)S(1)}, f32[4,4]{1,0:T(4,128)S(1)}) custom-call(f32[64,1,384]{2,1,0:T(1,128)} %x_in.1, s32[1,1,8]{2,1,0:T(1,128)} %wall_cell_in.1, s32[1,1]{1,0:T(1,128)S(6)} %copy.17.wall_count_in, s32[1,1,8]{2,1,0:T(1,128)} %wall_panel_in.1, f32[2,3072]{1,0:T(2,128)} %left_in.1, f32[2,3072]{1,0:T(2,128)} %right_in.1, ...), custom_call_target="tpu_custom_call" | custom-call | flops 1000000000 | bytes 2000000 | tf_op jit(solution)/shard_map/collide/pallas_call | solution.py:648
  52.3 0.6 %copy.15 = f32[64,1,384]{2,1,0:T(1,128)} copy(f32[64,1,384]{2,1,0:T(1,128)S(1)} %get-tuple-element.2) | data formatting | bytes 196608
  52.9 0.6 %copy.16 = f32[4,4]{1,0:T(4,128)} copy(f32[4,4]{1,0:T(4,128)S(1)} %get-tuple-element.3) | data formatting | bytes 128

commit v8 on v6

--- a/solution.py
+++ b/solution.py
@@ -551,7 +551,7 @@
     def send_home(to, column):
         send_block(packed_back, arrived_back, 1, to, to, me_y)
 
-    in_place_order(send_home, 0, ring // 4)
+    in_place_order(send_home, 0, 1)
 
     both = low + high
     sums_low, sums_high = jnp.sum(low, axis=0), jnp.sum(high, axis=0)
@@ -590,7 +590,7 @@
     lax.fori_loop(1, cells, give, 0)
     pl.when(moved_home)(lambda: give(0, None))
 
-    in_place_order(send_home, ring // 4, ring)
+    in_place_order(send_home, 1, ring)
     arrived_back[pl.ds(me_y, 1)] = packed_back[pl.ds(me_v, 1)]
 
     @pl.when(moved_home)

time: 51.2 us -> 50.7 us (level)
  no operation moved by 1% of the time
where the time goes in v8:
time: 50.7 us; the launch traced here: 50.3 us
  Pallas kernels  47.8 us (94%)
  between operations  1.29 us (3%)
  local copies, waits for them, and re-layouts  1.22 us (2%)
    pallas_call x1, Pallas kernels, per_device(): pl.pallas_call(functools.partial(kernel, cells, columns), out_shape=(pltp...  47.8 us
    unnamed x2, local copies, waits for them, and re-layouts  1.22 us

profile of v8, /device:TPU:1, one launch (start us, length us, event | category | flops | bytes accessed | tf_op | source)
XLA Modules:
  0.0 50.3 jit_solution(8011088520776207610)
XLA Ops:
  1.3 47.8 %collide.1 = (f32[64,1,384]{2,1,0:T(1,128)S(1)}, f32[4,4]{1,0:T(4,128)S(1)}) custom-call(f32[64,1,384]{2,1,0:T(1,128)} %x_in.1, s32[1,1,8]{2,1,0:T(1,128)} %wall_cell_in.1, s32[1,1]{1,0:T(1,128)S(6)} %copy.17.wall_count_in, s32[1,1,8]{2,1,0:T(1,128)} %wall_panel_in.1, f32[2,3072]{1,0:T(2,128)} %left_in.1, f32[2,3072]{1,0:T(2,128)} %right_in.1, ...), custom_call_target="tpu_custom_call" | custom-call | flops 1000000000 | bytes 2000000 | tf_op jit(solution)/shard_map/collide/pallas_call | solution.py:647
  49.1 0.6 %copy.15 = f32[64,1,384]{2,1,0:T(1,128)} copy(f32[64,1,384]{2,1,0:T(1,128)S(1)} %get-tuple-element.2) | data formatting | bytes 196608
  49.7 0.6 %copy.16 = f32[4,4]{1,0:T(4,128)} copy(f32[4,4]{1,0:T(4,128)S(1)} %get-tuple-element.3) | data formatting | bytes 128
